TPU v7x, 32 devices: a whole 2x2x4 slice. The times are simulated.
32 devices in a mesh: dp: 8 (over z, y), seq: 4 (over x, core).
Axes of the slice: x: 2, y: 2, z: 4, core: 2. Of those that a mesh axis runs over, the one named last changes fastest.
Arguments:
- activations: bfloat16 [16384, 5120], P(('dp', 'seq')), may hold values from -6 to 6
- out_grads: bfloat16 [16384, 5120], P(('dp', 'seq')), may hold values from -6 to 6
- proj_in: bfloat16 [64, 5120], replicated, may hold values from -0.078125 to 0.078125
- proj_out: bfloat16 [128, 5120], replicated, may hold values from -0.078125 to 0.078125
- queries: float32 [128, 8192], P(('dp', 'seq')), may hold values from -3 to 3
- basis_a: float32 [64, 64], replicated, may hold values from -0.75 to 0.75
- basis_g: float32 [128, 128], replicated, may hold values from -0.5 to 0.5
- eigen: float32 [64, 128], replicated, may hold values from 0.05 to 5
- spans: int32 [8, 4, 4], P('dp'), may hold values from 1 to 320, 512 in all within a row
- doc_owner: int32 [8, 4], P('dp'), may hold values from 0 to 7, as said below
- doc_lengths: int32 [8, 4], P('dp'), may hold values from 1280 to 5120
Outputs:
- influence: float32 [8, 8, 128], P('dp', None, 'seq')
Inputs may be any that keep to these rules, and one draw needn't show every extreme that they name: In every row spans[j, s, :] the 4 entries sum to 512, and the largest is exactly 320. The 4 owners in each row doc_owner[j, :] differ from one another, and one owner is named in every row.
All inputs are finite; a program needn't handle non-finite values.
Results may differ from a plain program's by a relative error of at most 0.0058.
Values may be sent and summed in bfloat16 or wider, within the bound.
No kernel may reach another device: no remote copies, remote signals or barrier semaphores. Data moves between devices by JAX's collectives and lax.ppermute only.
A program may use at most 64 MiB of HBM per device.

v0:
```python
import jax
import jax.numpy as jnp
from jax import lax
from jax.sharding import PartitionSpec as P

damping = 0.1


def project(act_rows, grad_rows, proj_in, proj_out):
    contract = (((1,), (1,)), ((), ()))
    a_part = lax.dot_general(
        act_rows, proj_in, contract, preferred_element_type=jnp.float32
    ).astype(jnp.bfloat16)
    g_part = lax.dot_general(
        grad_rows, proj_out, contract, preferred_element_type=jnp.float32
    ).astype(jnp.bfloat16)
    return jnp.concatenate([a_part, g_part], axis=1)


def doc_terms(features, starts, span_ends, input_width):
    row_count = features.shape[0]
    position = lax.broadcasted_iota(jnp.int32, (1, 1, row_count), 2)
    inside = (position >= starts[:, :, None]) & (position < span_ends[:, :, None])
    member = jnp.sum(inside.astype(jnp.int32), axis=0).astype(jnp.bfloat16)
    a_part = jnp.transpose(features[:, :input_width])
    g_part = features[:, input_width:]
    spread = member[:, None, :] * a_part[None, :, :]
    flattened = spread.reshape(-1, row_count)
    summed = jnp.dot(flattened, g_part, preferred_element_type=jnp.float32)
    return summed.reshape(member.shape[0], -1)


def whiten(queries, basis_a, basis_g, eigen):
    highest = lax.Precision.HIGHEST
    input_width = basis_a.shape[0]
    output_width = basis_g.shape[0]
    query_grid = queries.reshape(-1, input_width, output_width)
    half_turn = jnp.einsum("ai,nab->nib", basis_a, query_grid, precision=highest)
    rotated = jnp.einsum("nib,bc->nic", half_turn, basis_g, precision=highest)
    scaled = rotated / (eigen + damping)
    returned = jnp.einsum("ai,nic->nac", basis_a, scaled, precision=highest)
    whitened = jnp.einsum("nac,bc->nab", returned, basis_g, precision=highest)
    return whitened.reshape(-1, input_width * output_width).astype(jnp.bfloat16)


def per_device(
    activations,
    out_grads,
    proj_in,
    proj_out,
    queries,
    basis_a,
    basis_g,
    eigen,
    spans,
    doc_owner,
    doc_lengths,
):
    n_dp = lax.axis_size("dp")
    input_width = basis_a.shape[0]
    my_index = lax.axis_index("seq")
    span_row = spans[0]
    features = project(activations, out_grads, proj_in, proj_out)
    own_span = lax.dynamic_index_in_dim(span_row, my_index, 0, keepdims=False)
    span_ends = jnp.cumsum(own_span)
    starts = span_ends - own_span
    partial_value = doc_terms(features, starts[None, :], span_ends[None, :], input_width)
    doc_sum = lax.psum_scatter(partial_value, "seq", scatter_dimension=1, tiled=True)
    doc_grad = (doc_sum / doc_lengths[0].astype(jnp.float32)[:, None]).astype(jnp.bfloat16)
    owners = doc_owner[0]
    select = (jnp.arange(n_dp, dtype=jnp.int32)[:, None] == owners[None, :]).astype(jnp.bfloat16)
    outgoing = jnp.dot(select, doc_grad, preferred_element_type=jnp.float32).astype(jnp.bfloat16)
    arrived = lax.all_to_all(outgoing, "dp", split_axis=0, concat_axis=0, tiled=True)
    whitened = whiten(queries, basis_a, basis_g, eigen)
    columns = lax.all_to_all(whitened, "seq", split_axis=1, concat_axis=0, tiled=True)
    contract = (((1,), (1,)), ((), ()))
    part = lax.dot_general(
        arrived,
        lax.all_gather(columns, "dp", axis=0, tiled=True),
        contract,
        preferred_element_type=jnp.float32,
    )
    summed = lax.psum_scatter(part, "seq", scatter_dimension=1, tiled=True)
    return summed.reshape(1, n_dp, -1)


def solution(mesh):
    return jax.shard_map(
        per_device,
        mesh=mesh,
        in_specs=(
            P(("dp", "seq"), None),
            P(("dp", "seq"), None),
            P(),
            P(),
            P(("dp", "seq"), None),
            P(),
            P(),
            P(),
            P("dp", None, None),
            P("dp", None),
            P("dp", None),
        ),
        out_specs=P("dp", None, "seq"),
        check_vma=False,
    )
```

profile of v0, /device:TPU:0, one launch (start us, length us, event | category | flops | bytes accessed | tf_op | source)
XLA Modules:
  0.0 136.8 jit_solution(10046603349072854607)
XLA Ops:
  6.5 0.8 fusion.13
  7.3 0.2 reduce-window.7
  7.5 0.7 bitcast_subtract_fusion
  8.2 0.1 convert_convert_fusion
  8.3 4.4 %convolution_convert_fusion.2 = bf16[64,512]{1,0:T(8,128)(2,1)S(1)} fusion(bf16[64,5120]{1,0:T(8,128)(2,1)} %param.13, bf16[512,5120]{1,0:T(8,128)(2,1)} %param.11), kind=kOutput, calls=%fused_computation.6 | convolution fusion | flops 335577088 | bytes 5963776 | tf_op jit(solution)/shard_map/dot_general | solution.py:11
  12.7 4.3 %fusion.1 = f32[256,128]{1,0:T(8,128)S(1)} fusion(bf16[256,512]{1,0:T(8,128)(2,1)S(1)} %bitcast.52, bf16[512,5120]{1,0:T(8,128)(2,1)} %param.12, bf16[128,5120]{1,0:T(8,128)(2,1)S(1)} %copy-done), kind=kOutput, calls=%fused_computation.9 | convolution fusion | flops 704708608 | bytes 6946816 | tf_op jit(solution)/shard_map/dot_general | solution.py:29
  17.0 0.0 copy-start.4
  17.0 0.0 copy-start.1
  17.0 0.0 copy-start.2
  17.0 0.0 copy-start.3
  17.1 2.6 %copy.21 = f32[4,8192]{0,1:T(8,128)} copy(f32[4,8192]{1,0:T(4,128)S(1)} %reshape.123) | data formatting | bytes 262144
  19.8 0.0 reduce-scatter.7.cloned.1.call-update
  19.8 0.3 convolution_bitcast_fusion.1
  20.2 0.3 convolution_divide_fusion
  20.4 0.3 convolution_bitcast_fusion
  20.7 0.3 convolution_convert_fusion.3
  21.0 0.7 copy.18
  21.7 4.2 %all-to-all-start.1 = ((bf16[4,4,2048]{2,0,1:T(4,128)(2,1)}), bf16[4,4,2048]{2,0,1:T(4,128)(2,1)S(1)}, u32[]{:S(2)}, u32[]{:S(2)}) async-start(bf16[4,4,2048]{2,0,1:T(4,128)(2,1)} %copy.18), calls=%async_computation.1 | async-start | bytes 131072 | tf_op jit(solution)/shard_map/all_to_all | solution.py:75
  25.9 4.1 %all-to-all-done.1 = bf16[4,4,2048]{2,0,1:T(4,128)(2,1)S(1)} async-done(((bf16[4,4,2048]{2,0,1:T(4,128)(2,1)}), bf16[4,4,2048]{2,0,1:T(4,128)(2,1)S(1)}, u32[]{:S(2)}, u32[]{:S(2)}) %all-to-all-start.1) | async-done | bytes 65568 | tf_op jit(solution)/shard_map/all_to_all | solution.py:75
  30.0 37.1 %reduce-scatter.7.cloned.1.call-done = f32[2048,4]{1,0:T(8,128)} async-done(((f32[8192,4]{1,0:T(8,128)}), f32[2048,4]{1,0:T(8,128)}) %reduce-scatter.7.cloned.1.call-update) | async-done | bytes 32784
  67.2 1.6 %copy.22 = f32[4,2048]{1,0:T(4,128)S(1)} copy(f32[4,2048]{0,1:T(8,128)} %bitcast.51) | data formatting | bytes 65536
  68.7 0.2 fusion
  68.9 0.5 broadcast.33
  69.4 0.7 reduce
  70.1 0.6 reshape.133
  70.7 5.5 %all-to-all-start = ((bf16[8,2,1024]{2,1,0:T(2,128)(2,1)}), bf16[8,2,1024]{2,1,0:T(2,128)(2,1)S(1)}, u32[]{:S(2)}, u32[]{:S(2)}) async-start(bf16[8,2,1024]{2,1,0:T(2,128)(2,1)} %reshape.133), calls=%async_computation | async-start | bytes 65536 | tf_op jit(solution)/shard_map/all_to_all | solution.py:73
  76.2 0.0 reduce-scatter.9.cloned.1.call-start
  76.3 31.9 %all_gather.3 = bf16[128,2048]{1,0:T(8,128)(2,1)S(1)} all-gather(bf16[16,2048]{1,0:T(8,128)(2,1)S(1)} %all_to_all.25), channel_id=1, replica_groups=mesh['dp'=8,'seq'=4] {'dp'}, dimensions={0}, use_global_device_ids=true | all-gather | bytes 589824 | tf_op jit(solution)/shard_map/all_gather | solution.py:79
  108.2 0.9 convolution_bitcast_fusion.2
  109.1 0.0 reduce-scatter.9.cloned.1.call-update
  109.1 19.5 %reduce-scatter.9.cloned.1.call-done = f32[32,8]{1,0:T(8,128)} async-done(((f32[128,8]{1,0:T(8,128)}), f32[32,8]{1,0:T(8,128)}) %reduce-scatter.9.cloned.1.call-update) | async-done | bytes 1040
  128.6 1.4 %copy.24 = f32[8,32]{1,0:T(8,128)} copy(f32[8,32]{0,1:T(8,128)} %bitcast.55) | data formatting | bytes 2048
  (19 shorter events, 0.2 us)
Async XLA Ops:
  6.5 6.2 %copy-start = (bf16[128,5120]{1,0:T(8,128)(2,1)S(1)}, bf16[128,5120]{1,0:T(8,128)(2,1)}, u32[]{:S(2)}) copy-start(bf16[128,5120]{1,0:T(8,128)(2,1)} %param.14) | copy-start | bytes 3932164
  6.5 60.6 %reduce-scatter.7.cloned.1.call-start = ((), (), s32[]{:S(2)}) async-start(), calls=%async_computation.4 | async-start | bytes 5242880
  17.0 2.8 %copy-start.4 = (f32[64,128]{1,0:T(8,128)S(1)}, f32[64,128]{1,0:T(8,128)}, u32[]{:S(2)}) copy-start(f32[64,128]{1,0:T(8,128)} %param.18) | copy-start | bytes 98308
  17.0 2.8 %copy-start.1 = (f32[64,64]{1,0:T(8,128)S(1)}, f32[64,64]{1,0:T(8,128)}, u32[]{:S(2)}) copy-start(f32[64,64]{1,0:T(8,128)} %param.16) | copy-start | bytes 49156
  17.0 2.8 %copy-start.2 = (f32[4,8192]{1,0:T(4,128)S(1)}, f32[4,8192]{1,0:T(4,128)}, u32[]{:S(2)}) copy-start(f32[4,8192]{1,0:T(4,128)} %param.15) | copy-start | bytes 393220
  17.0 3.1 %copy-start.3 = (f32[128,128]{1,0:T(8,128)S(1)}, f32[128,128]{1,0:T(8,128)}, u32[]{:S(2)}) copy-start(f32[128,128]{1,0:T(8,128)} %param.17) | copy-start | bytes 196612
  17.0 8.8 %copy-start.5 = (s32[1,4]{1,0:T(1,128)S(1)}, s32[1,4]{1,0:T(1,128)}, u32[]{:S(2)}) copy-start(s32[1,4]{1,0:T(1,128)} %param.21) | copy-start | bytes 52
  17.1 51.6 %copy-start.6 = (s32[1,4]{1,0:T(1,128)S(1)}, s32[1,4]{1,0:T(1,128)}, u32[]{:S(2)}) copy-start(s32[1,4]{1,0:T(1,128)} %param.20) | copy-start | bytes 52
  21.7 8.3 %all-to-all-start.1 = ((bf16[4,4,2048]{2,0,1:T(4,128)(2,1)}), bf16[4,4,2048]{2,0,1:T(4,128)(2,1)S(1)}, u32[]{:S(2)}, u32[]{:S(2)}) async-start(bf16[4,4,2048]{2,0,1:T(4,128)(2,1)} %copy.18), calls=%async_computation.1 | async-start | bytes 131072 | tf_op jit(solution)/shard_map/all_to_all | solution.py:75
  70.7 37.4 %all-to-all-start = ((bf16[8,2,1024]{2,1,0:T(2,128)(2,1)}), bf16[8,2,1024]{2,1,0:T(2,128)(2,1)S(1)}, u32[]{:S(2)}, u32[]{:S(2)}) async-start(bf16[8,2,1024]{2,1,0:T(2,128)(2,1)} %reshape.133), calls=%async_computation | async-start | bytes 65536 | tf_op jit(solution)/shard_map/all_to_all | solution.py:73
  76.2 52.4 %reduce-scatter.9.cloned.1.call-start = ((), (), s32[]{:S(2)}) async-start(), calls=%async_computation.5 | async-start | bytes 81920
Sparse Core Ops, SparseCore 0:
  19.9 47.2 reduce-scatter.6
  109.2 19.3 reduce-scatter.8
where the time goes:
time: 137 us
  waiting for transfers between devices  60.8 us (44%)
  blocking collectives  31.9 us (23%)
  between operations  13.6 us (10%)
  matrix products  10.9 us (8%)
  starting transfers between devices  9.74 us (7%)
  local copies, waits for them, and re-layouts  8.32 us (6%)
  other arithmetic  1.63 us (1%)
    unnamed x4, waiting for transfers between devices  56.7 us
    all_gather x1, blocking collectives, per_device(): lax.all_gather(columns, 'dp', axis=0, tiled=True)  31.9 us
    unnamed x19, local copies, waits for them, and re-layouts  6.25 us
    all_to_all x1, starting transfers between devices, per_device(): lax.all_to_all(outgoing, 'dp', split_axis=0, concat_axis=0, tiled=True)  5.5 us
    dot_general x1, matrix products, project(): lax.dot_general(act_rows, proj_in, contract, preferred_element_type=jnp.f...  4.41 us
    dot_general x1, matrix products, doc_terms(): summed = jnp.dot(flattened, g_part, preferred_element_type=jnp.float32)  4.26 us
    all_to_all x1, starting transfers between devices, per_device(): lax.all_to_all(whitened, 'seq', split_axis=1, concat_axis=0, tiled=True)  4.2 us
    all_to_all x1, waiting for transfers between devices, per_device(): lax.all_to_all(whitened, 'seq', split_axis=1, concat_axis=0, tiled=True)  4.12 us
  transfers between devices with their start and end apart: 4, of which 3 were waited for; matrix products, arithmetic and copies ran while one was open for 1% of the time, Pallas kernels for 0%

commit v1 on v0

v1 whole, which is shorter than its diff:
```python
import functools

import jax
import jax.numpy as jnp
from jax import lax
from jax.experimental import pallas as pl
from jax.experimental.pallas import tpu as pltpu
from jax.sharding import PartitionSpec as P

damping = 0.1
vmem_bytes = 64 * 1024 * 1024
small_bytes = 16 * 1024 * 1024

NT = (((1,), (1,)), ((), ()))
NN = (((1,), (0,)), ((), ()))
TN = (((0,), (0,)), ((), ()))


def whiten_kernel(q_ref, ba_ref, bg_ref, eig_ref, out_ref, rows_ref):
    count = q_ref.shape[0]
    wa, wg = eig_ref.shape
    n_seq = out_ref.shape[1]
    share = wa // n_seq
    dot = functools.partial(
        lax.dot_general,
        precision=lax.Precision.HIGHEST,
        preferred_element_type=jnp.float32,
    )
    for a in range(wa):
        rows_ref[a * count : (a + 1) * count, :] = q_ref[:, a * wg : (a + 1) * wg]
    grid = jnp.concatenate(
        [rows_ref[pl.ds(n, wa, stride=count), :] for n in range(count)], axis=0
    )
    ba, bg = ba_ref[...], bg_ref[...]
    scale = eig_ref[...] + damping
    half = dot(grid, bg, NN)
    back = []
    for n in range(count):
        rotated = dot(ba, half[n * wa : (n + 1) * wa], TN)
        back.append(dot(ba, rotated / scale, NN))
    white = dot(jnp.concatenate(back, axis=0), bg, NT).astype(jnp.bfloat16)
    for n in range(count):
        for s in range(n_seq):
            lo = n * wa + s * share
            block = white[lo : lo + share]
            for o in range(out_ref.shape[0]):
                out_ref[o, s, n] = block


def docs_kernel(
    steps,
    span_hbm,
    owner_hbm,
    length_hbm,
    act_hbm,
    grad_hbm,
    pin_hbm,
    pout_hbm,
    after_hbm,
    out_ref,
    act,
    grad,
    pin,
    pout,
    span_ref,
    owner_ref,
    length_ref,
    sems,
    small_sems,
):
    rows, width = act_hbm.shape
    part = width // steps
    wa = pin_hbm.shape[0]
    n_docs = owner_ref.shape[1]
    n_seq, share, wg = out_ref.shape[1:]
    copies = []
    for k in range(steps):
        cols = pl.ds(k * part, part)
        step = []
        for i, (src, dst) in enumerate(
            ((pin_hbm, pin), (act_hbm, act), (pout_hbm, pout), (grad_hbm, grad))
        ):
            copy = pltpu.make_async_copy(src.at[:, cols], dst.at[k], sems.at[k, i])
            copy.start()
            step.append(copy)
        copies.append(step)
    small = []
    for i, (src, dst) in enumerate(
        ((span_hbm, span_ref), (owner_hbm, owner_ref), (length_hbm, length_ref))
    ):
        copy = pltpu.make_async_copy(src, dst, small_sems.at[i])
        copy.start()
        small.append(copy)
    a_sum = jnp.zeros((rows, wa), jnp.float32)
    g_sum = jnp.zeros((rows, wg), jnp.float32)
    for k in range(steps):
        copies[k][0].wait()
        copies[k][1].wait()
        a_sum += lax.dot_general(
            act[k], pin[k], NT, preferred_element_type=jnp.float32
        )
        copies[k][2].wait()
        copies[k][3].wait()
        g_sum += lax.dot_general(
            grad[k], pout[k], NT, preferred_element_type=jnp.float32
        )
    for copy in small:
        copy.wait()
    a_t = a_sum.T.astype(jnp.bfloat16).astype(jnp.float32)
    g_part = g_sum.astype(jnp.bfloat16)
    me = lax.axis_index("seq")
    position = lax.broadcasted_iota(jnp.int32, (wa, rows), 1)
    start = jnp.int32(0)
    spread = []
    for d in range(n_docs):
        end = start + span_ref[0, me, d]
        inside = (position >= start) & (position < end)
        spread.append(jnp.where(inside, a_t, 0.0).astype(jnp.bfloat16))
        start = end
    sums = jnp.dot(
        jnp.concatenate(spread, axis=0), g_part, preferred_element_type=jnp.float32
    )
    out_ref[...] = jnp.zeros_like(out_ref)
    for d in range(n_docs):
        length = jnp.full((wa, wg), length_ref[0, d], jnp.int32).astype(jnp.float32)
        doc = (sums[d * wa : (d + 1) * wa] / length).astype(jnp.bfloat16)
        out_ref[owner_ref[0, d]] = doc.reshape(n_seq, share, wg)


def score_kernel(docs_ref, white_ref, *refs):
    out_refs, sum_ref = refs[:-1], refs[-1]
    n_dp, n_seq, share, wg = docs_ref.shape
    count = white_ref.shape[0]
    n_out = out_refs[0].shape[1]
    width = n_dp * share
    total = docs_ref[:, 0].astype(jnp.float32)
    for s in range(1, n_seq):
        total += docs_ref[:, s].astype(jnp.float32)
    docs = total.reshape(width, wg).astype(jnp.bfloat16)
    white = white_ref[...].reshape(count * share, wg)
    cross = lax.dot_general(white, docs, NT, preferred_element_type=jnp.float32)
    cross = cross.reshape(count, share, width)
    row = lax.broadcasted_iota(jnp.int32, (share, width), 0)
    col = lax.broadcasted_iota(jnp.int32, (share, width), 1)
    same = (row == col % share)[None]
    sum_ref[...] = jnp.sum(jnp.where(same, cross, 0.0), axis=1)
    owner = lax.broadcasted_iota(jnp.int32, (n_dp, width), 0)
    lane = lax.broadcasted_iota(jnp.int32, (n_dp, width), 1)
    gather = (lane // share == owner).astype(jnp.float32)
    me = lax.axis_index("seq")
    for k in range(n_seq):
        block = sum_ref[pl.ds((me ^ k) * n_out, n_out), :]
        out_refs[k][...] = lax.dot_general(
            gather,
            block,
            NT,
            precision=lax.Precision.HIGHEST,
            preferred_element_type=jnp.float32,
        )


def column_chunks(width):
    weights = (5, 5, 4, 3, 2, 1)
    unit = width // sum(weights)
    if unit * sum(weights) != width or unit % 128:
        return ((0, width),)
    chunks, lo = [], 0
    for weight in weights:
        chunks.append((lo, lo + weight * unit))
        lo += weight * unit
    return tuple(chunks)


def features_kernel(chunks, n_dp, *refs):
    hbm_refs, out_ref, vmem_refs = refs[:11], refs[11], refs[12:23]
    rows_ref, order_ref, placed_ref, small_sems, sems = refs[23:]
    q, ba_ref, bg_ref, eig_ref, span, owner, length, act, grad, pin, pout = vmem_refs
    bf16, f32 = jnp.bfloat16, jnp.float32
    count = q.shape[0]
    wa, wg = eig_ref.shape
    rows = act.shape[0]
    n_docs = owner.shape[1]
    n_dev = n_dp * lax.axis_size("seq")
    height = out_ref.shape[0] // n_dev
    share = wa // n_dev
    high = functools.partial(
        lax.dot_general,
        precision=lax.Precision.HIGHEST,
        preferred_element_type=f32,
    )
    dot = functools.partial(lax.dot_general, preferred_element_type=f32)

    small = []
    for i in range(7):
        copy = pltpu.make_async_copy(hbm_refs[i], vmem_refs[i], small_sems.at[i])
        copy.start()
        small.append(copy)
    copies = []
    for k, (lo, hi) in enumerate(chunks):
        step = []
        for i in (2, 0, 3, 1):
            copy = pltpu.make_async_copy(
                hbm_refs[7 + i].at[:, lo:hi],
                vmem_refs[7 + i].at[:, lo:hi],
                sems.at[k, i],
            )
            copy.start()
            step.append(copy)
        copies.append(step)
    for copy in small:
        copy.wait()

    for a in range(wa):
        rows_ref[a * count : (a + 1) * count, :] = q[:, a * wg : (a + 1) * wg]
    grid = jnp.concatenate(
        [rows_ref[pl.ds(n, wa, stride=count), :] for n in range(count)], axis=0
    )
    ba, bg = ba_ref[...], bg_ref[...]
    scale = eig_ref[...] + damping
    half = high(grid, bg, NN)
    back = []
    for n in range(count):
        rotated = high(ba, half[n * wa : (n + 1) * wa], TN)
        back.append(high(ba, rotated / scale, NN))
    white = high(jnp.concatenate(back, axis=0), bg, NT).astype(bf16)

    def iota(width, dim):
        return lax.broadcasted_iota(jnp.int32, (height, width), dim)

    first = share * n_dp
    t, col = iota(count * wa, 0), iota(count * wa, 1)
    r, n = lax.div(t - first, count), lax.rem(t - first, count)
    fits = (t >= first) & (lax.div(col, wa) == n)
    base = jnp.where(fits, lax.rem(col, wa) - r, -1)
    picks = [(base == share * f).astype(f32) for f in range(n_dev)]
    order = jnp.concatenate(picks, axis=0).astype(bf16)
    placed_ref[...] = dot(order, white, NN)
    t, col = iota(n_docs * wa, 0), iota(n_docs * wa, 1)
    r, o = lax.div(t, n_dp), lax.rem(t, n_dp)
    doc = lax.div(col, wa)
    doc_owner = jnp.full_like(col, owner[0, 0])
    for d in range(1, n_docs):
        doc_owner = jnp.where(doc == d, owner[0, d], doc_owner)
    fits = (t < first) & (doc_owner == o)
    base = jnp.where(fits, lax.rem(col, wa) - r, -1)
    picks = [(base == share * f).astype(f32) for f in range(n_dev)]
    order_ref[...] = jnp.concatenate(picks, axis=0).astype(bf16)

    a_sum = jnp.zeros((wa, rows), f32)
    g_sum = jnp.zeros((wg, rows), f32)
    for k, (lo, hi) in enumerate(chunks):
        copies[k][0].wait()
        copies[k][1].wait()
        a_sum += dot(pin[:, lo:hi], act[:, lo:hi], NT)
        copies[k][2].wait()
        copies[k][3].wait()
        g_sum += dot(pout[:, lo:hi], grad[:, lo:hi], NT)
    a_part = a_sum.astype(bf16).astype(f32)
    g_part = g_sum.astype(bf16)
    me = lax.axis_index("seq")
    position = lax.broadcasted_iota(jnp.int32, (wa, rows), 1)
    start = jnp.int32(0)
    spread = []
    for d in range(n_docs):
        end = start + span[0, me, d]
        inside = (position >= start) & (position < end)
        spread.append(jnp.where(inside, a_part, 0.0).astype(bf16))
        start = end
    sums = dot(jnp.concatenate(spread, axis=0), g_part, NT)
    docs = []
    for d in range(n_docs):
        tokens = jnp.full((wa, wg), length[0, d], jnp.int32).astype(f32)
        docs.append((sums[d * wa : (d + 1) * wa] / tokens).astype(bf16))
    routed = dot(order_ref[...], jnp.concatenate(docs, axis=0), NN)
    out_ref[...] = (placed_ref[...] + routed).astype(bf16)


def partial_kernel(n_dp, count, block_ref, out_ref):
    bf16, f32 = jnp.bfloat16, jnp.float32
    n_seq = out_ref.shape[1]
    n_hi = out_ref.shape[2]
    n_dev = n_dp * n_seq
    rows, wg = block_ref.shape
    height = rows // n_dev
    share = height // (n_dp + count)
    n_out = n_dev * count // n_seq
    n_lo = n_dp // n_hi
    blocks = block_ref[...].astype(f32).reshape(n_dp, n_seq, height, wg)
    docs, white = [], []
    for r in range(share):
        lo = r * n_dp
        total = blocks[:, 0, lo : lo + n_dp]
        for s in range(1, n_seq):
            total += blocks[:, s, lo : lo + n_dp]
        docs.append(total.reshape(n_dp * n_dp, wg))
        lo = share * n_dp + r * count
        white.append(blocks[:, :, lo : lo + count].reshape(n_dev * count, wg))
    docs = jnp.concatenate(docs, axis=1)
    white = jnp.concatenate(white, axis=1).astype(bf16)
    upper = docs.astype(bf16)
    lower = (docs - upper.astype(f32)).astype(bf16)
    both = lax.dot_general(
        jnp.concatenate([upper, lower], axis=0), white, NT, preferred_element_type=f32
    )
    scores = both[: n_dp * n_dp] + both[n_dp * n_dp :]
    tall = n_hi * n_dp
    for s in range(n_seq):
        lanes = slice(s * n_out, (s + 1) * n_out)
        packed = jnp.concatenate(
            [scores[lo * tall : (lo + 1) * tall, lanes] for lo in range(n_lo)], axis=1
        )
        for hi in range(n_hi):
            out_ref[:, s, hi, :] = packed[hi * n_dp : (hi + 1) * n_dp]


def finish_kernel(parts_ref, out_ref):
    n_hi = parts_ref.shape[1]
    n_dp, n_out = out_ref.shape
    total = jnp.sum(parts_ref[...], axis=0)
    for lo in range(n_dp // n_hi):
        out_ref[lo * n_hi : (lo + 1) * n_hi, :] = total[:, lo * n_out : (lo + 1) * n_out]


def by_features(
    activations,
    out_grads,
    proj_in,
    proj_out,
    queries,
    basis_a,
    basis_g,
    eigen,
    spans,
    doc_owner,
    doc_lengths,
):
    n_dp, n_seq = lax.axis_size("dp"), lax.axis_size("seq")
    n_dev = n_dp * n_seq
    wa, wg = eigen.shape
    count = queries.shape[0]
    share = wa // n_dev
    height = share * (n_dp + count)
    n_out = n_dev * count // n_seq
    n_hi = n_dp * n_out // 128
    bf16, f32 = jnp.bfloat16, jnp.float32
    chunks = column_chunks(activations.shape[1])
    params = pltpu.CompilerParams(vmem_limit_bytes=vmem_bytes)
    vmem = pl.BlockSpec(memory_space=pltpu.VMEM)
    hbm = pl.BlockSpec(memory_space=pltpu.HBM)
    small = (queries, basis_a, basis_g, eigen)
    integers = (spans, doc_owner, doc_lengths)
    large = (activations, out_grads, proj_in, proj_out)
    copied = (
        [pltpu.VMEM(x.shape, x.dtype) for x in small]
        + [pltpu.SMEM(x.shape, x.dtype) for x in integers]
        + [pltpu.VMEM(x.shape, x.dtype) for x in large]
    )
    blocks = pl.pallas_call(
        functools.partial(features_kernel, chunks, n_dp),
        out_shape=jax.ShapeDtypeStruct((n_dev * height, wg), bf16),
        in_specs=[hbm] * 11,
        out_specs=vmem,
        scratch_shapes=copied
        + [
            pltpu.VMEM((wa * count, wg), f32),
            pltpu.VMEM((n_dev * height, doc_owner.shape[1] * wa), bf16),
            pltpu.VMEM((n_dev * height, wg), f32),
            pltpu.SemaphoreType.DMA((7,)),
            pltpu.SemaphoreType.DMA((len(chunks), 4)),
        ],
        compiler_params=params,
        name="features",
    )(*small, *integers, *large)
    everywhere = functools.partial(
        lax.all_to_all,
        axis_name=("dp", "seq"),
        split_axis=0,
        concat_axis=0,
        tiled=True,
    )
    blocks = everywhere(blocks)
    parts = pl.pallas_call(
        functools.partial(partial_kernel, n_dp, count),
        out_shape=jax.ShapeDtypeStruct((n_dp, n_seq, n_hi, 128), f32),
        in_specs=[vmem],
        out_specs=vmem,
        compiler_params=pltpu.CompilerParams(vmem_limit_bytes=small_bytes),
        name="partial",
    )(blocks)
    parts = everywhere(parts.reshape(n_dev, n_hi, 128))
    result = pl.pallas_call(
        finish_kernel,
        out_shape=jax.ShapeDtypeStruct((n_dp, n_out), f32),
        in_specs=[vmem],
        out_specs=vmem,
        compiler_params=pltpu.CompilerParams(vmem_limit_bytes=small_bytes),
        name="finish",
    )(parts)
    return result[None]


def by_rows(
    activations,
    out_grads,
    proj_in,
    proj_out,
    queries,
    basis_a,
    basis_g,
    eigen,
    spans,
    doc_owner,
    doc_lengths,
):
    n_dp, n_seq = lax.axis_size("dp"), lax.axis_size("seq")
    n_dev = n_dp * n_seq
    rows, width = activations.shape
    wa, wg = eigen.shape
    count = queries.shape[0]
    share = wa // n_seq
    steps = 5
    part = width // steps
    bf16, f32 = jnp.bfloat16, jnp.float32
    params = pltpu.CompilerParams(vmem_limit_bytes=vmem_bytes)
    vmem = pl.BlockSpec(memory_space=pltpu.VMEM)
    hbm = pl.BlockSpec(memory_space=pltpu.HBM)

    outgoing = pl.pallas_call(
        whiten_kernel,
        out_shape=jax.ShapeDtypeStruct((n_dp, n_seq, count, share, wg), bf16),
        in_specs=[vmem] * 4,
        out_specs=vmem,
        scratch_shapes=[pltpu.VMEM((wa * count, wg), f32)],
        compiler_params=params,
        name="whiten",
    )(queries, basis_a, basis_g, eigen)
    white = lax.all_to_all(
        outgoing.reshape(n_dev, count, share, wg),
        ("dp", "seq"),
        split_axis=0,
        concat_axis=0,
        tiled=True,
    )

    docs = pl.pallas_call(
        functools.partial(docs_kernel, steps),
        out_shape=jax.ShapeDtypeStruct((n_dp, n_seq, share, wg), bf16),
        in_specs=[hbm] * 8,
        out_specs=vmem,
        scratch_shapes=[
            pltpu.VMEM((steps, rows, part), bf16),
            pltpu.VMEM((steps, rows, part), bf16),
            pltpu.VMEM((steps, wa, part), bf16),
            pltpu.VMEM((steps, wg, part), bf16),
            pltpu.SMEM(spans.shape, jnp.int32),
            pltpu.SMEM(doc_owner.shape, jnp.int32),
            pltpu.SMEM(doc_lengths.shape, jnp.int32),
            pltpu.SemaphoreType.DMA((steps, 4)),
            pltpu.SemaphoreType.DMA((3,)),
        ],
        compiler_params=params,
        name="docs",
    )(
        spans,
        doc_owner,
        doc_lengths,
        activations,
        out_grads,
        proj_in,
        proj_out,
        outgoing,
    )
    docs = lax.all_to_all(
        docs.reshape(n_dev, share, wg),
        ("dp", "seq"),
        split_axis=0,
        concat_axis=0,
        tiled=True,
    )

    n_query = n_dev * count
    n_out = n_query // n_seq
    parts = pl.pallas_call(
        score_kernel,
        out_shape=[jax.ShapeDtypeStruct((n_dp, n_out), f32)] * n_seq,
        in_specs=[vmem] * 2,
        out_specs=[vmem] * n_seq,
        scratch_shapes=[pltpu.VMEM((n_query, n_dp * share), f32)],
        compiler_params=params,
        name="score",
    )(docs.reshape(n_dp, n_seq, share, wg), white.reshape(n_query, share, wg))
    result = parts[0]
    for k in range(n_seq - 1, 0, -1):
        pairs = [(i, i ^ k) for i in range(n_seq)]
        result = result + lax.ppermute(parts[k], "seq", pairs)
    return result[None]


def per_device(*args):
    n_dp, n_seq = lax.axis_size("dp"), lax.axis_size("seq")
    n_dev = n_dp * n_seq
    wa, wg = args[7].shape
    count = args[4].shape[0]
    share = wa // n_dev
    n_out = n_dp * count
    fits = (
        share * n_dev == wa
        and wg == 128
        and n_dp % 8 == 0
        and share * count % 8 == 0
        and 128 % n_out == 0
        and n_dp * n_out % 128 == 0
    )
    return (by_features if fits else by_rows)(*args)


def solution(mesh):
    return jax.shard_map(
        per_device,
        mesh=mesh,
        in_specs=(
            P(("dp", "seq"), None),
            P(("dp", "seq"), None),
            P(),
            P(),
            P(("dp", "seq"), None),
            P(),
            P(),
            P(),
            P("dp", None, None),
            P("dp", None),
            P("dp", None),
        ),
        out_specs=P("dp", None, "seq"),
        check_vma=False,
    )
```

time: 137 us -> 38.7 us (0.28)
  waiting for transfers between devices: 60.8 us -> 0 us
  between operations: 13.6 us -> 0.02 us
  Pallas kernels: 0 us -> 12.5 us
  matrix products: 10.9 us -> 0 us
  starting transfers between devices: 9.74 us -> 0 us
  local copies, waits for them, and re-layouts: 8.32 us -> 0 us
  blocking collectives: 31.9 us -> 26 us
  other arithmetic: 1.63 us -> 0 us
    unnamed x4 -> x0, waiting for transfers between devices: 56.7 us -> none
    all_gather x1 -> x0, blocking collectives: 31.9 us -> none  [per_device(): lax.all_gather(columns, 'dp', axis=0, tiled=True)]
    all_to_all x0 -> x2, blocking collectives: none -> 26 us  [the longest x1 16.2 us: by_features(): blocks = everywhere(blocks)]
    pallas_call x0 -> x3, Pallas kernels: none -> 12.5 us  [the longest x1 11.5 us: by_features(): pl.pallas_call(functools.partial(features_kernel, chunks, n_dp), out_shap...]
    dot_general x7 -> x0, matrix products: 9.99 us -> none  [the longest x1 4.41 us: project(): lax.dot_general(act_rows, proj_in, contract, preferred_element_type=jnp.f...]
    all_to_all x2 -> x0, starting transfers between devices: 9.7 us -> none  [the longest x1 5.5 us: per_device(): lax.all_to_all(outgoing, 'dp', split_axis=0, concat_axis=0, tiled=True)]
    unnamed x19 -> x0, local copies, waits for them, and re-layouts: 6.25 us -> none
    all_to_all x2 -> x0, waiting for transfers between devices: 4.12 us -> none  [the longest x1 4.12 us: per_device(): lax.all_to_all(whitened, 'seq', split_axis=1, concat_axis=0, tiled=True)]
  transfers between devices with their start and end apart: 4 -> 0, of which waited for: 3 -> 0; matrix products, arithmetic and copies ran while one was open for 1% -> 0% of each run, Pallas kernels for 0% -> 0%
where the time goes in v1:
time: 38.7 us; the launch traced here: 38.5 us
  blocking collectives  26 us (67%)
  Pallas kernels  12.5 us (32%)
    all_to_all x1, blocking collectives, by_features(): blocks = everywhere(blocks)  16.2 us
    pallas_call x1, Pallas kernels, by_features(): pl.pallas_call(functools.partial(features_kernel, chunks, n_dp), out_shap...  11.5 us
    all_to_all x1, blocking collectives, by_features(): parts = everywhere(parts.reshape(n_dev, n_hi, 128))  9.77 us

profile of v1, /device:TPU:0, one launch (start us, length us, event | category | flops | bytes accessed | tf_op | source)
XLA Modules:
  0.0 38.5 jit_solution(14181599940313659389)
XLA Ops:
  0.0 11.5 %features.1 = bf16[768,128]{1,0:T(8,128)(2,1)} custom-call(f32[4,8192]{1,0:T(4,128)} %refs_0_.1, f32[64,64]{1,0:T(8,128)} %refs_1_.1, f32[128,128]{1,0:T(8,128)} %refs_2_.1, f32[64,128]{1,0:T(8,128)} %refs_3_.1, s32[1,4,4]{2,1,0:T(4,128)} %refs_4_.1, s32[1,4]{1,0:T(1,128)} %refs_5_.1, s32[1,4]{1,0:T(1,128)} %refs_6_.1, bf16[512,5120]{1,0:T(8,128)(2,1)} %refs_7_.1, ...), custom_call_target="tpu_custom_call" | custom-call | tf_op jit(solution)/shard_map/features/pallas_call | solution.py:358
  11.6 16.2 %all_to_all.16 = bf16[32,24,128]{2,1,0:T(8,128)(2,1)S(1)} all-to-all(bf16[32,24,128]{2,1,0:T(8,128)(2,1)} %bitcast.6), channel_id=1, replica_groups=mesh['dp'=8,'seq'=4] {'dp','seq'}, dimensions={0} | all-to-all | bytes 393216 | tf_op jit(solution)/shard_map/all_to_all | solution.py:381
  27.8 0.3 partial.1
  28.0 9.8 %all_to_all.17.parts_ref = f32[32,2,128]{2,1,0:T(2,128)S(1)} all-to-all(f32[32,2,128]{2,1,0:T(2,128)S(1)} %bitcast.5), channel_id=1, replica_groups=mesh['dp'=8,'seq'=4] {'dp','seq'}, dimensions={0} | all-to-all | bytes 65536 | tf_op jit(solution)/shard_map/all_to_all | solution.py:390
  37.8 0.7 %finish.1 = f32[8,32]{1,0:T(8,128)} custom-call(f32[32,2,128]{2,1,0:T(2,128)S(1)} %all_to_all.17.parts_ref), custom_call_target="tpu_custom_call" | custom-call | tf_op jit(solution)/shard_map/finish/pallas_call | solution.py:391

commit v2 on v1

--- a/solution.py
+++ b/solution.py
@@ -159,104 +159,94 @@
         )
 
 
-def column_chunks(width):
-    weights = (5, 5, 4, 3, 2, 1)
-    unit = width // sum(weights)
-    if unit * sum(weights) != width or unit % 128:
-        return ((0, width),)
-    chunks, lo = [], 0
-    for weight in weights:
-        chunks.append((lo, lo + weight * unit))
-        lo += weight * unit
-    return tuple(chunks)
-
-
-def features_kernel(chunks, n_dp, *refs):
-    hbm_refs, out_ref, vmem_refs = refs[:11], refs[11], refs[12:23]
-    rows_ref, order_ref, placed_ref, small_sems, sems = refs[23:]
-    q, ba_ref, bg_ref, eig_ref, span, owner, length, act, grad, pin, pout = vmem_refs
+def split_dot(x, w):
+    bf16 = jnp.bfloat16
+    x_hi, w_hi = x.astype(bf16), w.astype(bf16)
+    x_lo = (x - x_hi.astype(jnp.float32)).astype(bf16)
+    w_lo = (w - w_hi.astype(jnp.float32)).astype(bf16)
+    return jnp.dot(
+        jnp.concatenate([x_hi, x_lo, x_hi], axis=1),
+        jnp.concatenate([w_hi, w_hi, w_lo], axis=0),
+        preferred_element_type=jnp.float32,
+    )
+
+
+def side_by_side(x, count):
+    rows = x.shape[0] // count
+    return jnp.concatenate(
+        [x[n * rows : (n + 1) * rows] for n in range(count)], axis=1
+    )
+
+
+def features_kernel(steps, n_dp, *refs):
+    hbm_refs, out_ref, local_refs = refs[:11], refs[11], refs[12:23]
+    rows_ref, a_sum, g_sum, blocks, small_sems, sems = refs[23:]
+    q, ba_ref, bg_ref, eig_ref, span, owner, length, act, grad, pin, pout = local_refs
     bf16, f32 = jnp.bfloat16, jnp.float32
     count = q.shape[0]
     wa, wg = eig_ref.shape
-    rows = act.shape[0]
+    rows, part = act.shape[1:]
     n_docs = owner.shape[1]
-    n_dev = n_dp * lax.axis_size("seq")
-    height = out_ref.shape[0] // n_dev
+    n_dev = out_ref.shape[0]
     share = wa // n_dev
-    high = functools.partial(
-        lax.dot_general,
-        precision=lax.Precision.HIGHEST,
-        preferred_element_type=f32,
-    )
     dot = functools.partial(lax.dot_general, preferred_element_type=f32)
+
+    def chunk(k):
+        cols = pl.ds(pl.multiple_of(k * part, part), part)
+        return [
+            pltpu.make_async_copy(
+                hbm_refs[7 + i].at[:, cols], local_refs[7 + i].at[k], sems.at[k, i]
+            )
+            for i in (2, 0, 3, 1)
+        ]
 
     small = []
     for i in range(7):
-        copy = pltpu.make_async_copy(hbm_refs[i], vmem_refs[i], small_sems.at[i])
+        copy = pltpu.make_async_copy(hbm_refs[i], local_refs[i], small_sems.at[i])
         copy.start()
         small.append(copy)
-    copies = []
-    for k, (lo, hi) in enumerate(chunks):
-        step = []
-        for i in (2, 0, 3, 1):
-            copy = pltpu.make_async_copy(
-                hbm_refs[7 + i].at[:, lo:hi],
-                vmem_refs[7 + i].at[:, lo:hi],
-                sems.at[k, i],
-            )
-            copy.start()
-            step.append(copy)
-        copies.append(step)
-    for copy in small:
+    for copy in chunk(0):
+        copy.start()
+    a_sum[...] = jnp.zeros_like(a_sum)
+    g_sum[...] = jnp.zeros_like(g_sum)
+    blocks[: share * n_dp] = jnp.zeros_like(blocks[: share * n_dp])
+    def whiten():
+        for copy in small[:4]:
+            copy.wait()
+        for k in range(1, steps):
+            for copy in chunk(k):
+                copy.start()
+        for a in range(wa):
+            rows_ref[a * count : (a + 1) * count, :] = q[:, a * wg : (a + 1) * wg]
+        grid = jnp.concatenate(
+            [rows_ref[pl.ds(n, wa, stride=count), :] for n in range(count)], axis=0
+        )
+        ba, bg = ba_ref[...], bg_ref[...]
+        scale = jnp.concatenate([eig_ref[...] + damping] * count, axis=1)
+        rotated = split_dot(ba.T, side_by_side(split_dot(grid, bg), count))
+        back = split_dot(ba, rotated / scale)
+        back = jnp.concatenate(
+            [back[:, n * wg : (n + 1) * wg] for n in range(count)], axis=0
+        )
+        white = split_dot(back, bg.T)
+        for r in range(share):
+            for n in range(count):
+                lo = n * wa + r * n_dev
+                blocks[share * n_dp + r * count + n] = white[lo : lo + n_dev]
+
+    def add_chunk(k, carry):
+        for copy in chunk(k):
+            copy.wait()
+        a_sum[...] += dot(act[k], pin[k], NT)
+        g_sum[...] += dot(grad[k], pout[k], NT)
+        return carry
+
+    whiten()
+    lax.fori_loop(0, steps, add_chunk, 0)
+    for copy in small[4:]:
         copy.wait()
-
-    for a in range(wa):
-        rows_ref[a * count : (a + 1) * count, :] = q[:, a * wg : (a + 1) * wg]
-    grid = jnp.concatenate(
-        [rows_ref[pl.ds(n, wa, stride=count), :] for n in range(count)], axis=0
-    )
-    ba, bg = ba_ref[...], bg_ref[...]
-    scale = eig_ref[...] + damping
-    half = high(grid, bg, NN)
-    back = []
-    for n in range(count):
-        rotated = high(ba, half[n * wa : (n + 1) * wa], TN)
-        back.append(high(ba, rotated / scale, NN))
-    white = high(jnp.concatenate(back, axis=0), bg, NT).astype(bf16)
-
-    def iota(width, dim):
-        return lax.broadcasted_iota(jnp.int32, (height, width), dim)
-
-    first = share * n_dp
-    t, col = iota(count * wa, 0), iota(count * wa, 1)
-    r, n = lax.div(t - first, count), lax.rem(t - first, count)
-    fits = (t >= first) & (lax.div(col, wa) == n)
-    base = jnp.where(fits, lax.rem(col, wa) - r, -1)
-    picks = [(base == share * f).astype(f32) for f in range(n_dev)]
-    order = jnp.concatenate(picks, axis=0).astype(bf16)
-    placed_ref[...] = dot(order, white, NN)
-    t, col = iota(n_docs * wa, 0), iota(n_docs * wa, 1)
-    r, o = lax.div(t, n_dp), lax.rem(t, n_dp)
-    doc = lax.div(col, wa)
-    doc_owner = jnp.full_like(col, owner[0, 0])
-    for d in range(1, n_docs):
-        doc_owner = jnp.where(doc == d, owner[0, d], doc_owner)
-    fits = (t < first) & (doc_owner == o)
-    base = jnp.where(fits, lax.rem(col, wa) - r, -1)
-    picks = [(base == share * f).astype(f32) for f in range(n_dev)]
-    order_ref[...] = jnp.concatenate(picks, axis=0).astype(bf16)
-
-    a_sum = jnp.zeros((wa, rows), f32)
-    g_sum = jnp.zeros((wg, rows), f32)
-    for k, (lo, hi) in enumerate(chunks):
-        copies[k][0].wait()
-        copies[k][1].wait()
-        a_sum += dot(pin[:, lo:hi], act[:, lo:hi], NT)
-        copies[k][2].wait()
-        copies[k][3].wait()
-        g_sum += dot(pout[:, lo:hi], grad[:, lo:hi], NT)
-    a_part = a_sum.astype(bf16).astype(f32)
-    g_part = g_sum.astype(bf16)
+    a_part = a_sum[...].T.astype(bf16).astype(f32)
+    g_part = g_sum[...].astype(bf16)
     me = lax.axis_index("seq")
     position = lax.broadcasted_iota(jnp.int32, (wa, rows), 1)
     start = jnp.int32(0)
@@ -266,13 +256,13 @@
         inside = (position >= start) & (position < end)
         spread.append(jnp.where(inside, a_part, 0.0).astype(bf16))
         start = end
-    sums = dot(jnp.concatenate(spread, axis=0), g_part, NT)
-    docs = []
+    sums = dot(jnp.concatenate(spread, axis=0), g_part, NN)
     for d in range(n_docs):
-        tokens = jnp.full((wa, wg), length[0, d], jnp.int32).astype(f32)
-        docs.append((sums[d * wa : (d + 1) * wa] / tokens).astype(bf16))
-    routed = dot(order_ref[...], jnp.concatenate(docs, axis=0), NN)
-    out_ref[...] = (placed_ref[...] + routed).astype(bf16)
+        tokens = jnp.full((n_dev, wg), length[0, d], jnp.int32).astype(f32)
+        for r in range(share):
+            lo = d * wa + r * n_dev
+            blocks[r * n_dp + owner[0, d]] = sums[lo : lo + n_dev] / tokens
+    out_ref[...] = jnp.swapaxes(blocks[...], 0, 1).astype(bf16)
 
 
 def partial_kernel(n_dp, count, block_ref, out_ref):
@@ -280,8 +270,7 @@
     n_seq = out_ref.shape[1]
     n_hi = out_ref.shape[2]
     n_dev = n_dp * n_seq
-    rows, wg = block_ref.shape
-    height = rows // n_dev
+    height, wg = block_ref.shape[1:]
     share = height // (n_dp + count)
     n_out = n_dev * count // n_seq
     n_lo = n_dp // n_hi
@@ -343,7 +332,8 @@
     n_out = n_dev * count // n_seq
     n_hi = n_dp * n_out // 128
     bf16, f32 = jnp.bfloat16, jnp.float32
-    chunks = column_chunks(activations.shape[1])
+    steps = 5
+    part = activations.shape[1] // steps
     params = pltpu.CompilerParams(vmem_limit_bytes=vmem_bytes)
     vmem = pl.BlockSpec(memory_space=pltpu.VMEM)
     hbm = pl.BlockSpec(memory_space=pltpu.HBM)
@@ -353,20 +343,21 @@
     copied = (
         [pltpu.VMEM(x.shape, x.dtype) for x in small]
         + [pltpu.SMEM(x.shape, x.dtype) for x in integers]
-        + [pltpu.VMEM(x.shape, x.dtype) for x in large]
+        + [pltpu.VMEM((steps, x.shape[0], part), x.dtype) for x in large]
     )
     blocks = pl.pallas_call(
-        functools.partial(features_kernel, chunks, n_dp),
-        out_shape=jax.ShapeDtypeStruct((n_dev * height, wg), bf16),
+        functools.partial(features_kernel, steps, n_dp),
+        out_shape=jax.ShapeDtypeStruct((n_dev, height, wg), bf16),
         in_specs=[hbm] * 11,
         out_specs=vmem,
         scratch_shapes=copied
         + [
             pltpu.VMEM((wa * count, wg), f32),
-            pltpu.VMEM((n_dev * height, doc_owner.shape[1] * wa), bf16),
-            pltpu.VMEM((n_dev * height, wg), f32),
+            pltpu.VMEM((activations.shape[0], wa), f32),
+            pltpu.VMEM((activations.shape[0], wg), f32),
+            pltpu.VMEM((height, n_dev, wg), f32),
             pltpu.SemaphoreType.DMA((7,)),
-            pltpu.SemaphoreType.DMA((len(chunks), 4)),
+            pltpu.SemaphoreType.DMA((steps, 4)),
         ],
         compiler_params=params,
         name="features",

time: 38.7 us -> 34.1 us (0.88)
  Pallas kernels: 12.5 us -> 7.87 us
    pallas_call x1, Pallas kernels: 11.5 us -> 6.92 us  [by_features(): pl.pallas_call(functools.partial(features_kernel, steps, n_dp), out_shape...]
where the time goes in v2:
time: 34.1 us; the launch traced here: 33.9 us
  blocking collectives  26 us (76%)
  Pallas kernels  7.87 us (23%)
    all_to_all x1, blocking collectives, by_features(): blocks = everywhere(blocks)  16.2 us
    all_to_all x1, blocking collectives, by_features(): parts = everywhere(parts.reshape(n_dev, n_hi, 128))  9.77 us
    pallas_call x1, Pallas kernels, by_features(): pl.pallas_call(functools.partial(features_kernel, steps, n_dp), out_shape...  6.92 us
    pallas_call x1, Pallas kernels, by_features(): pl.pallas_call(finish_kernel, out_shape=jax.ShapeDtypeStruct((n_dp, n_out...  0.7 us

profile of v2, /device:TPU:0, one launch (start us, length us, event | category | flops | bytes accessed | tf_op | source)
XLA Modules:
  0.0 33.9 jit_solution(6712215377602213194)
XLA Ops:
  0.0 6.9 %features.1 = bf16[32,24,128]{2,1,0:T(8,128)(2,1)} custom-call(f32[4,8192]{1,0:T(4,128)} %refs_0_.1, f32[64,64]{1,0:T(8,128)} %refs_1_.1, f32[128,128]{1,0:T(8,128)} %refs_2_.1, f32[64,128]{1,0:T(8,128)} %refs_3_.1, s32[1,4,4]{2,1,0:T(4,128)} %refs_4_.1, s32[1,4]{1,0:T(1,128)} %refs_5_.1, s32[1,4]{1,0:T(1,128)} %refs_6_.1, bf16[512,5120]{1,0:T(8,128)(2,1)} %refs_7_.1, ...), custom_call_target="tpu_custom_call" | custom-call | tf_op jit(solution)/shard_map/features/pallas_call | solution.py:348
  6.9 16.2 %all_to_all.10.block_ref = bf16[32,24,128]{2,1,0:T(8,128)(2,1)S(1)} all-to-all(bf16[32,24,128]{2,1,0:T(8,128)(2,1)} %features.1), channel_id=1, replica_groups=mesh['dp'=8,'seq'=4] {'dp','seq'}, dimensions={0} | all-to-all | bytes 393216 | tf_op jit(solution)/shard_map/all_to_all | solution.py:372
  23.1 0.3 partial.1
  23.4 9.8 %all_to_all.11.parts_ref = f32[32,2,128]{2,1,0:T(2,128)S(1)} all-to-all(f32[32,2,128]{2,1,0:T(2,128)S(1)} %bitcast.2), channel_id=1, replica_groups=mesh['dp'=8,'seq'=4] {'dp','seq'}, dimensions={0} | all-to-all | bytes 65536 | tf_op jit(solution)/shard_map/all_to_all | solution.py:381
  33.2 0.7 %finish.1 = f32[8,32]{1,0:T(8,128)} custom-call(f32[32,2,128]{2,1,0:T(2,128)S(1)} %all_to_all.11.parts_ref), custom_call_target="tpu_custom_call" | custom-call | tf_op jit(solution)/shard_map/finish/pallas_call | solution.py:382

commit v3 on v2

--- a/solution.py
+++ b/solution.py
@@ -178,7 +178,7 @@
     )
 
 
-def features_kernel(steps, n_dp, *refs):
+def features_kernel(steps, *refs):
     hbm_refs, out_ref, local_refs = refs[:11], refs[11], refs[12:23]
     rows_ref, a_sum, g_sum, blocks, small_sems, sems = refs[23:]
     q, ba_ref, bg_ref, eig_ref, span, owner, length, act, grad, pin, pout = local_refs
@@ -209,7 +209,6 @@
         copy.start()
     a_sum[...] = jnp.zeros_like(a_sum)
     g_sum[...] = jnp.zeros_like(g_sum)
-    blocks[: share * n_dp] = jnp.zeros_like(blocks[: share * n_dp])
     def whiten():
         for copy in small[:4]:
             copy.wait()
@@ -232,7 +231,7 @@
         for r in range(share):
             for n in range(count):
                 lo = n * wa + r * n_dev
-                blocks[share * n_dp + r * count + n] = white[lo : lo + n_dev]
+                blocks[share * n_docs + r * count + n] = white[lo : lo + n_dev]
 
     def add_chunk(k, carry):
         for copy in chunk(k):
@@ -261,29 +260,36 @@
         tokens = jnp.full((n_dev, wg), length[0, d], jnp.int32).astype(f32)
         for r in range(share):
             lo = d * wa + r * n_dev
-            blocks[r * n_dp + owner[0, d]] = sums[lo : lo + n_dev] / tokens
-    out_ref[...] = jnp.swapaxes(blocks[...], 0, 1).astype(bf16)
-
-
-def partial_kernel(n_dp, count, block_ref, out_ref):
+            blocks[r * n_docs + d] = sums[lo : lo + n_dev] / tokens
+        target = jnp.full((n_dev, wg), owner[0, d], jnp.int32).astype(f32)
+        blocks[share * (n_docs + count) + d] = target
+    table = jnp.swapaxes(blocks[...], 0, 1)
+    for i in range(out_ref.shape[1]):
+        out_ref[:, i] = table[:, i * n_docs : (i + 1) * n_docs].astype(bf16)
+
+
+def partial_kernel(block_ref, out_ref, rows_ref):
     bf16, f32 = jnp.bfloat16, jnp.float32
-    n_seq = out_ref.shape[1]
-    n_hi = out_ref.shape[2]
-    n_dev = n_dp * n_seq
-    height, wg = block_ref.shape[1:]
-    share = height // (n_dp + count)
+    n_dp, n_seq, n_hi = out_ref.shape[:3]
+    n_dev, groups, n_docs, wg = block_ref.shape
+    share = groups // 2
+    count = n_docs
     n_out = n_dev * count // n_seq
     n_lo = n_dp // n_hi
-    blocks = block_ref[...].astype(f32).reshape(n_dp, n_seq, height, wg)
     docs, white = [], []
     for r in range(share):
-        lo = r * n_dp
-        total = blocks[:, 0, lo : lo + n_dp]
+        part = block_ref[:, r].astype(f32).reshape(n_dp, n_seq, n_docs, wg)
+        total = part[:, 0]
         for s in range(1, n_seq):
-            total += blocks[:, s, lo : lo + n_dp]
-        docs.append(total.reshape(n_dp * n_dp, wg))
-        lo = share * n_dp + r * count
-        white.append(blocks[:, :, lo : lo + count].reshape(n_dev * count, wg))
+            total += part[:, s]
+        rows_ref[r] = total
+        docs.append(
+            jnp.concatenate([rows_ref[r, :, d] for d in range(n_docs)], axis=0)
+        )
+        white.append(block_ref[:, share + r].astype(f32).reshape(n_dev * count, wg))
+    rows_ref[share] = (
+        block_ref[:, 2 * share].astype(f32).reshape(n_dp, n_seq, n_docs, wg)[:, 0]
+    )
     docs = jnp.concatenate(docs, axis=1)
     white = jnp.concatenate(white, axis=1).astype(bf16)
     upper = docs.astype(bf16)
@@ -291,7 +297,19 @@
     both = lax.dot_general(
         jnp.concatenate([upper, lower], axis=0), white, NT, preferred_element_type=f32
     )
-    scores = both[: n_dp * n_dp] + both[n_dp * n_dp :]
+    scores = both[: n_docs * n_dp] + both[n_docs * n_dp :]
+    owners = [
+        jnp.broadcast_to(rows_ref[share, :, d][:, :1], (n_dp, n_dev * count))
+        for d in range(n_docs)
+    ]
+    routed = []
+    for o in range(n_dp):
+        row = jnp.zeros((n_dp, n_dev * count), f32)
+        for d in range(n_docs):
+            mine = owners[d] == float(o)
+            row += jnp.where(mine, scores[d * n_dp : (d + 1) * n_dp], 0.0)
+        routed.append(row)
+    scores = jnp.swapaxes(jnp.stack(routed), 0, 1).reshape(n_dp * n_dp, n_dev * count)
     tall = n_hi * n_dp
     for s in range(n_seq):
         lanes = slice(s * n_out, (s + 1) * n_out)
@@ -328,7 +346,8 @@
     wa, wg = eigen.shape
     count = queries.shape[0]
     share = wa // n_dev
-    height = share * (n_dp + count)
+    n_docs = doc_owner.shape[1]
+    height = share * (n_docs + count) + n_docs
     n_out = n_dev * count // n_seq
     n_hi = n_dp * n_out // 128
     bf16, f32 = jnp.bfloat16, jnp.float32
@@ -346,8 +365,8 @@
         + [pltpu.VMEM((steps, x.shape[0], part), x.dtype) for x in large]
     )
     blocks = pl.pallas_call(
-        functools.partial(features_kernel, steps, n_dp),
-        out_shape=jax.ShapeDtypeStruct((n_dev, height, wg), bf16),
+        functools.partial(features_kernel, steps),
+        out_shape=jax.ShapeDtypeStruct((n_dev, height // n_docs, n_docs, wg), bf16),
         in_specs=[hbm] * 11,
         out_specs=vmem,
         scratch_shapes=copied
@@ -371,10 +390,11 @@
     )
     blocks = everywhere(blocks)
     parts = pl.pallas_call(
-        functools.partial(partial_kernel, n_dp, count),
+        partial_kernel,
         out_shape=jax.ShapeDtypeStruct((n_dp, n_seq, n_hi, 128), f32),
         in_specs=[vmem],
         out_specs=vmem,
+        scratch_shapes=[pltpu.VMEM((share + 1, n_dp, n_docs, wg), f32)],
         compiler_params=pltpu.CompilerParams(vmem_limit_bytes=small_bytes),
         name="partial",
     )(blocks)
@@ -498,7 +518,8 @@
         share * n_dev == wa
         and wg == 128
         and n_dp % 8 == 0
-        and share * count % 8 == 0
+        and n_dp <= 256
+        and args[9].shape[1] == count == 4
         and 128 % n_out == 0
         and n_dp * n_out % 128 == 0
     )

time: 34.1 us -> 33.5 us (0.982)
  blocking collectives: 26 us -> 25.3 us
    all_to_all x1, blocking collectives: 9.77 us -> 9.38 us  [by_features(): parts = everywhere(parts.reshape(n_dev, n_hi, 128))]
where the time goes in v3:
time: 33.5 us; the launch traced here: 33.3 us
  blocking collectives  25.3 us (76%)
  Pallas kernels  7.97 us (24%)
    all_to_all x1, blocking collectives, by_features(): blocks = everywhere(blocks)  15.9 us
    all_to_all x1, blocking collectives, by_features(): parts = everywhere(parts.reshape(n_dev, n_hi, 128))  9.38 us
    pallas_call x1, Pallas kernels, by_features(): pl.pallas_call(functools.partial(features_kernel, steps), out_shape=jax.S...  6.89 us
    pallas_call x1, Pallas kernels, by_features(): pl.pallas_call(finish_kernel, out_shape=jax.ShapeDtypeStruct((n_dp, n_out...  0.7 us

profile of v3, /device:TPU:0, one launch (start us, length us, event | category | flops | bytes accessed | tf_op | source)
XLA Modules:
  0.0 33.3 jit_solution(17562992635446652044)
XLA Ops:
  0.0 6.9 %features.1 = bf16[32,5,4,128]{3,2,1,0:T(4,128)(2,1)} custom-call(f32[4,8192]{1,0:T(4,128)} %refs_0_.1, f32[64,64]{1,0:T(8,128)} %refs_1_.1, f32[128,128]{1,0:T(8,128)} %refs_2_.1, f32[64,128]{1,0:T(8,128)} %refs_3_.1, s32[1,4,4]{2,1,0:T(4,128)} %refs_4_.1, s32[1,4]{1,0:T(1,128)} %refs_5_.1, s32[1,4]{1,0:T(1,128)} %refs_6_.1, bf16[512,5120]{1,0:T(8,128)(2,1)} %refs_7_.1, ...), custom_call_target="tpu_custom_call" | custom-call | tf_op jit(solution)/shard_map/features/pallas_call | solution.py:367
  6.9 15.9 %all_to_all.10.block_ref = bf16[32,5,4,128]{3,2,1,0:T(4,128)(2,1)S(1)} all-to-all(bf16[32,5,4,128]{3,2,1,0:T(4,128)(2,1)} %features.1), channel_id=1, replica_groups=mesh['dp'=8,'seq'=4] {'dp','seq'}, dimensions={0} | all-to-all | bytes 327680 | tf_op jit(solution)/shard_map/all_to_all | solution.py:391
  22.8 0.4 %partial.1 = f32[8,4,2,128]{3,2,1,0:T(2,128)S(1)} custom-call(bf16[32,5,4,128]{3,2,1,0:T(4,128)(2,1)S(1)} %all_to_all.10.block_ref), custom_call_target="tpu_custom_call" | custom-call | tf_op jit(solution)/shard_map/partial/pallas_call | solution.py:392
  23.2 9.4 %all_to_all.11.parts_ref = f32[32,2,128]{2,1,0:T(2,128)S(1)} all-to-all(f32[32,2,128]{2,1,0:T(2,128)S(1)} %bitcast.2), channel_id=1, replica_groups=mesh['dp'=8,'seq'=4] {'dp','seq'}, dimensions={0} | all-to-all | bytes 65536 | tf_op jit(solution)/shard_map/all_to_all | solution.py:401
  32.6 0.7 %finish.1 = f32[8,32]{1,0:T(8,128)} custom-call(f32[32,2,128]{2,1,0:T(2,128)S(1)} %all_to_all.11.parts_ref), custom_call_target="tpu_custom_call" | custom-call | tf_op jit(solution)/shard_map/finish/pallas_call | solution.py:402

commit v4 on v3

--- a/solution.py
+++ b/solution.py
@@ -205,16 +205,14 @@
         copy = pltpu.make_async_copy(hbm_refs[i], local_refs[i], small_sems.at[i])
         copy.start()
         small.append(copy)
-    for copy in chunk(0):
-        copy.start()
+    for k in range(steps):
+        for copy in chunk(k):
+            copy.start(priority=1)
     a_sum[...] = jnp.zeros_like(a_sum)
     g_sum[...] = jnp.zeros_like(g_sum)
     def whiten():
         for copy in small[:4]:
             copy.wait()
-        for k in range(1, steps):
-            for copy in chunk(k):
-                copy.start()
         for a in range(wa):
             rows_ref[a * count : (a + 1) * count, :] = q[:, a * wg : (a + 1) * wg]
         grid = jnp.concatenate(
@@ -231,7 +229,7 @@
         for r in range(share):
             for n in range(count):
                 lo = n * wa + r * n_dev
-                blocks[share * n_docs + r * count + n] = white[lo : lo + n_dev]
+                blocks[(n_docs + n) * share + r] = white[lo : lo + n_dev]
 
     def add_chunk(k, carry):
         for copy in chunk(k):
@@ -260,48 +258,56 @@
         tokens = jnp.full((n_dev, wg), length[0, d], jnp.int32).astype(f32)
         for r in range(share):
             lo = d * wa + r * n_dev
-            blocks[r * n_docs + d] = sums[lo : lo + n_dev] / tokens
-        target = jnp.full((n_dev, wg), owner[0, d], jnp.int32).astype(f32)
-        blocks[share * (n_docs + count) + d] = target
+            blocks[d * share + r] = sums[lo : lo + n_dev] / tokens
+    lane = lax.broadcasted_iota(jnp.int32, (n_dev, wg), 1)
+    each = n_docs // share
+    for r in range(share):
+        target = jnp.full((n_dev, wg), owner[0, r * each], jnp.int32)
+        for i in range(1, each):
+            target = jnp.where(lane >= i * (wg // each), owner[0, r * each + i], target)
+        blocks[(n_docs + count) * share + r] = target.astype(f32)
     table = jnp.swapaxes(blocks[...], 0, 1)
     for i in range(out_ref.shape[1]):
-        out_ref[:, i] = table[:, i * n_docs : (i + 1) * n_docs].astype(bf16)
-
-
-def partial_kernel(block_ref, out_ref, rows_ref):
+        out_ref[:, i] = table[:, i * share : (i + 1) * share].astype(bf16)
+
+
+def partial_kernel(n_docs, block_ref, out_ref, rows_ref, white_ref):
     bf16, f32 = jnp.bfloat16, jnp.float32
     n_dp, n_seq, n_hi = out_ref.shape[:3]
-    n_dev, groups, n_docs, wg = block_ref.shape
-    share = groups // 2
-    count = n_docs
+    n_dev, slots, share, wg = block_ref.shape
+    count = slots - n_docs - 1
     n_out = n_dev * count // n_seq
     n_lo = n_dp // n_hi
-    docs, white = [], []
-    for r in range(share):
-        part = block_ref[:, r].astype(f32).reshape(n_dp, n_seq, n_docs, wg)
+    docs = []
+    for d in range(n_docs):
+        part = block_ref[:, d].astype(f32).reshape(n_dp, n_seq, share, wg)
         total = part[:, 0]
         for s in range(1, n_seq):
             total += part[:, s]
-        rows_ref[r] = total
+        rows_ref[:n_dp] = total
         docs.append(
-            jnp.concatenate([rows_ref[r, :, d] for d in range(n_docs)], axis=0)
-        )
-        white.append(block_ref[:, share + r].astype(f32).reshape(n_dev * count, wg))
-    rows_ref[share] = (
-        block_ref[:, 2 * share].astype(f32).reshape(n_dp, n_seq, n_docs, wg)[:, 0]
-    )
-    docs = jnp.concatenate(docs, axis=1)
-    white = jnp.concatenate(white, axis=1).astype(bf16)
+            jnp.concatenate([rows_ref[:n_dp, r] for r in range(share)], axis=1)
+        )
+    docs = jnp.concatenate(docs, axis=0)
+    for n in range(count):
+        rows_ref[...] = block_ref[:, n_docs + n].astype(f32)
+        for r in range(share):
+            white_ref[r, pl.ds(n, n_dev, stride=count), :] = rows_ref[:, r]
+    white = jnp.concatenate([white_ref[r] for r in range(share)], axis=1).astype(bf16)
+    part = block_ref[:, n_docs + count].astype(f32)
+    rows_ref[:n_dp] = part.reshape(n_dp, n_seq, share, wg)[:, 0]
+    each = n_docs // share
+    owners = []
+    for d in range(n_docs):
+        lane = d % each * (wg // each)
+        column = rows_ref[:n_dp, d // each][:, lane : lane + 1]
+        owners.append(jnp.broadcast_to(column, (n_dp, n_dev * count)))
     upper = docs.astype(bf16)
     lower = (docs - upper.astype(f32)).astype(bf16)
     both = lax.dot_general(
         jnp.concatenate([upper, lower], axis=0), white, NT, preferred_element_type=f32
     )
     scores = both[: n_docs * n_dp] + both[n_docs * n_dp :]
-    owners = [
-        jnp.broadcast_to(rows_ref[share, :, d][:, :1], (n_dp, n_dev * count))
-        for d in range(n_docs)
-    ]
     routed = []
     for o in range(n_dp):
         row = jnp.zeros((n_dp, n_dev * count), f32)
@@ -347,7 +353,7 @@
     count = queries.shape[0]
     share = wa // n_dev
     n_docs = doc_owner.shape[1]
-    height = share * (n_docs + count) + n_docs
+    height = share * (n_docs + count + 1)
     n_out = n_dev * count // n_seq
     n_hi = n_dp * n_out // 128
     bf16, f32 = jnp.bfloat16, jnp.float32
@@ -366,7 +372,7 @@
     )
     blocks = pl.pallas_call(
         functools.partial(features_kernel, steps),
-        out_shape=jax.ShapeDtypeStruct((n_dev, height // n_docs, n_docs, wg), bf16),
+        out_shape=jax.ShapeDtypeStruct((n_dev, height // share, share, wg), bf16),
         in_specs=[hbm] * 11,
         out_specs=vmem,
         scratch_shapes=copied
@@ -390,11 +396,14 @@
     )
     blocks = everywhere(blocks)
     parts = pl.pallas_call(
-        partial_kernel,
+        functools.partial(partial_kernel, n_docs),
         out_shape=jax.ShapeDtypeStruct((n_dp, n_seq, n_hi, 128), f32),
         in_specs=[vmem],
         out_specs=vmem,
-        scratch_shapes=[pltpu.VMEM((share + 1, n_dp, n_docs, wg), f32)],
+        scratch_shapes=[
+            pltpu.VMEM((n_dev, share, wg), f32),
+            pltpu.VMEM((share, n_dev * count, wg), f32),
+        ],
         compiler_params=pltpu.CompilerParams(vmem_limit_bytes=small_bytes),
         name="partial",
     )(blocks)
@@ -515,11 +524,12 @@
     share = wa // n_dev
     n_out = n_dp * count
     fits = (
-        share * n_dev == wa
+        share > 0
+        and share * n_dev == wa
         and wg == 128
         and n_dp % 8 == 0
         and n_dp <= 256
-        and args[9].shape[1] == count == 4
+        and args[9].shape[1] % share == 0
         and 128 % n_out == 0
         and n_dp * n_out % 128 == 0
     )

time: 33.5 us -> 33.1 us (0.988)
  blocking collectives: 25.3 us -> 24.9 us
where the time goes in v4:
time: 33.1 us; the launch traced here: 32.9 us
  blocking collectives  24.9 us (75%)
  Pallas kernels  7.99 us (24%)
    all_to_all x1, blocking collectives, by_features(): blocks = everywhere(blocks)  15.7 us
    all_to_all x1, blocking collectives, by_features(): parts = everywhere(parts.reshape(n_dev, n_hi, 128))  9.19 us
    pallas_call x1, Pallas kernels, by_features(): pl.pallas_call(functools.partial(features_kernel, steps), out_shape=jax.S...  6.75 us
    pallas_call x1, Pallas kernels, by_features(): pl.pallas_call(finish_kernel, out_shape=jax.ShapeDtypeStruct((n_dp, n_out...  0.7 us

profile of v4, /device:TPU:0, one launch (start us, length us, event | category | flops | bytes accessed | tf_op | source)
XLA Modules:
  0.0 32.9 jit_solution(15370083594720927820)
XLA Ops:
  0.0 6.7 %features.1 = bf16[32,9,2,128]{3,2,1,0:T(2,128)(2,1)} custom-call(f32[4,8192]{1,0:T(4,128)} %refs_0_.1, f32[64,64]{1,0:T(8,128)} %refs_1_.1, f32[128,128]{1,0:T(8,128)} %refs_2_.1, f32[64,128]{1,0:T(8,128)} %refs_3_.1, s32[1,4,4]{2,1,0:T(4,128)} %refs_4_.1, s32[1,4]{1,0:T(1,128)} %refs_5_.1, s32[1,4]{1,0:T(1,128)} %refs_6_.1, bf16[512,5120]{1,0:T(8,128)(2,1)} %refs_7_.1, ...), custom_call_target="tpu_custom_call" | custom-call | tf_op jit(solution)/shard_map/features/pallas_call | solution.py:373
  6.8 15.7 %all_to_all.10.block_ref = bf16[32,9,2,128]{3,2,1,0:T(2,128)(2,1)S(1)} all-to-all(bf16[32,9,2,128]{3,2,1,0:T(2,128)(2,1)} %features.1), channel_id=1, replica_groups=mesh['dp'=8,'seq'=4] {'dp','seq'}, dimensions={0} | all-to-all | bytes 294912 | tf_op jit(solution)/shard_map/all_to_all | solution.py:397
  22.5 0.6 %partial.1 = f32[8,4,2,128]{3,2,1,0:T(2,128)S(1)} custom-call(bf16[32,9,2,128]{3,2,1,0:T(2,128)(2,1)S(1)} %all_to_all.10.block_ref), custom_call_target="tpu_custom_call" | custom-call | tf_op jit(solution)/shard_map/partial/pallas_call | solution.py:398
  23.0 9.2 %all_to_all.11.parts_ref = f32[32,2,128]{2,1,0:T(2,128)S(1)} all-to-all(f32[32,2,128]{2,1,0:T(2,128)S(1)} %bitcast.2), channel_id=1, replica_groups=mesh['dp'=8,'seq'=4] {'dp','seq'}, dimensions={0} | all-to-all | bytes 65536 | tf_op jit(solution)/shard_map/all_to_all | solution.py:410
  32.2 0.7 %finish.1 = f32[8,32]{1,0:T(8,128)} custom-call(f32[32,2,128]{2,1,0:T(2,128)S(1)} %all_to_all.11.parts_ref), custom_call_target="tpu_custom_call" | custom-call | tf_op jit(solution)/shard_map/finish/pallas_call | solution.py:411

commit v5 on v4

--- a/solution.py
+++ b/solution.py
@@ -9,6 +9,7 @@
 
 damping = 0.1
 vmem_bytes = 64 * 1024 * 1024
+features_bytes = 32 * 1024 * 1024
 small_bytes = 16 * 1024 * 1024
 
 NT = (((1,), (1,)), ((), ()))
@@ -359,12 +360,12 @@
     bf16, f32 = jnp.bfloat16, jnp.float32
     steps = 5
     part = activations.shape[1] // steps
-    params = pltpu.CompilerParams(vmem_limit_bytes=vmem_bytes)
     vmem = pl.BlockSpec(memory_space=pltpu.VMEM)
     hbm = pl.BlockSpec(memory_space=pltpu.HBM)
     small = (queries, basis_a, basis_g, eigen)
     integers = (spans, doc_owner, doc_lengths)
     large = (activations, out_grads, proj_in, proj_out)
+    operands = small + integers + large
     copied = (
         [pltpu.VMEM(x.shape, x.dtype) for x in small]
         + [pltpu.SMEM(x.shape, x.dtype) for x in integers]
@@ -384,9 +385,9 @@
             pltpu.SemaphoreType.DMA((7,)),
             pltpu.SemaphoreType.DMA((steps, 4)),
         ],
-        compiler_params=params,
+        compiler_params=pltpu.CompilerParams(vmem_limit_bytes=features_bytes),
         name="features",
-    )(*small, *integers, *large)
+    )(*(pltpu.with_memory_space_constraint(x, pltpu.HBM) for x in operands))
     everywhere = functools.partial(
         lax.all_to_all,
         axis_name=("dp", "seq"),

time: 33.1 us -> 32.2 us (0.973)
  Pallas kernels: 7.99 us -> 7.34 us
    pallas_call x1, Pallas kernels: 6.75 us -> 6.1 us  [by_features(): pl.pallas_call(functools.partial(features_kernel, steps), out_shape=jax.S...]
where the time goes in v5:
time: 32.2 us; the launch traced here: 32.1 us
  blocking collectives  24.7 us (77%)
  Pallas kernels  7.34 us (23%)
    all_to_all x1, blocking collectives, by_features(): blocks = everywhere(blocks)  15.5 us
    all_to_all x1, blocking collectives, by_features(): parts = everywhere(parts.reshape(n_dev, n_hi, 128))  9.19 us
    pallas_call x1, Pallas kernels, by_features(): pl.pallas_call(functools.partial(features_kernel, steps), out_shape=jax.S...  6.1 us
    pallas_call x1, Pallas kernels, by_features(): pl.pallas_call(finish_kernel, out_shape=jax.ShapeDtypeStruct((n_dp, n_out...  0.7 us

profile of v5, /device:TPU:0, one launch (start us, length us, event | category | flops | bytes accessed | tf_op | source)
XLA Modules:
  0.0 32.1 jit_solution(6982687817606072230)
XLA Ops:
  0.0 6.1 %features.1 = bf16[32,9,2,128]{3,2,1,0:T(2,128)(2,1)S(1)} custom-call(f32[4,8192]{1,0:T(4,128)} %refs_0_.1, f32[64,64]{1,0:T(8,128)} %refs_1_.1, f32[128,128]{1,0:T(8,128)} %refs_2_.1, f32[64,128]{1,0:T(8,128)} %refs_3_.1, s32[1,4,4]{2,1,0:T(4,128)} %refs_4_.1, s32[1,4]{1,0:T(1,128)} %refs_5_.1, s32[1,4]{1,0:T(1,128)} %refs_6_.1, bf16[512,5120]{1,0:T(8,128)(2,1)} %refs_7_.1, ...), custom_call_target="tpu_custom_call" | custom-call | tf_op jit(solution)/shard_map/features/pallas_call | solution.py:374
  6.1 15.5 %all_to_all.10.block_ref = bf16[32,9,2,128]{3,2,1,0:T(2,128)(2,1)S(1)} all-to-all(bf16[32,9,2,128]{3,2,1,0:T(2,128)(2,1)S(1)} %features.1), channel_id=1, replica_groups=mesh['dp'=8,'seq'=4] {'dp','seq'}, dimensions={0} | all-to-all | bytes 294912 | tf_op jit(solution)/shard_map/all_to_all | solution.py:398
  21.6 0.6 %partial.1 = f32[8,4,2,128]{3,2,1,0:T(2,128)S(1)} custom-call(bf16[32,9,2,128]{3,2,1,0:T(2,128)(2,1)S(1)} %all_to_all.10.block_ref), custom_call_target="tpu_custom_call" | custom-call | tf_op jit(solution)/shard_map/partial/pallas_call | solution.py:399
  22.2 9.2 %all_to_all.11.parts_ref = f32[32,2,128]{2,1,0:T(2,128)S(1)} all-to-all(f32[32,2,128]{2,1,0:T(2,128)S(1)} %bitcast.2), channel_id=1, replica_groups=mesh['dp'=8,'seq'=4] {'dp','seq'}, dimensions={0} | all-to-all | bytes 65536 | tf_op jit(solution)/shard_map/all_to_all | solution.py:411
  31.4 0.7 %finish.1 = f32[8,32]{1,0:T(8,128)} custom-call(f32[32,2,128]{2,1,0:T(2,128)S(1)} %all_to_all.11.parts_ref), custom_call_target="tpu_custom_call" | custom-call | tf_op jit(solution)/shard_map/finish/pallas_call | solution.py:412

commit v6 on v5

--- a/solution.py
+++ b/solution.py
@@ -211,6 +211,13 @@
             copy.start(priority=1)
     a_sum[...] = jnp.zeros_like(a_sum)
     g_sum[...] = jnp.zeros_like(g_sum)
+
+    def write_tiles(first, tiles):
+        table = jnp.swapaxes(blocks[: tiles * share], 0, 1)
+        for i in range(tiles):
+            tile = table[:, i * share : (i + 1) * share]
+            out_ref[:, first + i] = tile.astype(bf16)
+
     def whiten():
         for copy in small[:4]:
             copy.wait()
@@ -230,7 +237,8 @@
         for r in range(share):
             for n in range(count):
                 lo = n * wa + r * n_dev
-                blocks[(n_docs + n) * share + r] = white[lo : lo + n_dev]
+                blocks[n * share + r] = white[lo : lo + n_dev]
+        write_tiles(n_docs, count)
 
     def add_chunk(k, carry):
         for copy in chunk(k):
@@ -240,9 +248,18 @@
         return carry
 
     whiten()
-    lax.fori_loop(0, steps, add_chunk, 0)
     for copy in small[4:]:
         copy.wait()
+    row = lax.broadcasted_iota(jnp.int32, (share, wg), 0)
+    lane = lax.broadcasted_iota(jnp.int32, (share, wg), 1)
+    each = n_docs // share
+    place = row * each + lax.div(lane, wg // each)
+    target = jnp.full((share, wg), owner[0, 0], jnp.int32)
+    for d in range(1, n_docs):
+        target = jnp.where(place == d, owner[0, d], target)
+    target = jnp.broadcast_to(target.astype(f32)[None], (n_dev, share, wg))
+    out_ref[:, n_docs + count] = target.astype(bf16)
+    lax.fori_loop(0, steps, add_chunk, 0)
     a_part = a_sum[...].T.astype(bf16).astype(f32)
     g_part = g_sum[...].astype(bf16)
     me = lax.axis_index("seq")
@@ -260,16 +277,7 @@
         for r in range(share):
             lo = d * wa + r * n_dev
             blocks[d * share + r] = sums[lo : lo + n_dev] / tokens
-    lane = lax.broadcasted_iota(jnp.int32, (n_dev, wg), 1)
-    each = n_docs // share
-    for r in range(share):
-        target = jnp.full((n_dev, wg), owner[0, r * each], jnp.int32)
-        for i in range(1, each):
-            target = jnp.where(lane >= i * (wg // each), owner[0, r * each + i], target)
-        blocks[(n_docs + count) * share + r] = target.astype(f32)
-    table = jnp.swapaxes(blocks[...], 0, 1)
-    for i in range(out_ref.shape[1]):
-        out_ref[:, i] = table[:, i * share : (i + 1) * share].astype(bf16)
+    write_tiles(0, n_docs)
 
 
 def partial_kernel(n_docs, block_ref, out_ref, rows_ref, white_ref):
@@ -279,29 +287,32 @@
     count = slots - n_docs - 1
     n_out = n_dev * count // n_seq
     n_lo = n_dp // n_hi
-    docs = []
     for d in range(n_docs):
         part = block_ref[:, d].astype(f32).reshape(n_dp, n_seq, share, wg)
         total = part[:, 0]
         for s in range(1, n_seq):
             total += part[:, s]
-        rows_ref[:n_dp] = total
-        docs.append(
-            jnp.concatenate([rows_ref[:n_dp, r] for r in range(share)], axis=1)
-        )
-    docs = jnp.concatenate(docs, axis=0)
+        rows_ref[d, :n_dp] = total
+    for n in range(n_docs, n_docs + count):
+        rows_ref[n] = block_ref[:, n].astype(f32)
+    part = block_ref[:, n_docs + count].astype(f32)
+    rows_ref[n_docs + count, :n_dp] = part.reshape(n_dp, n_seq, share, wg)[:, 0]
     for n in range(count):
-        rows_ref[...] = block_ref[:, n_docs + n].astype(f32)
         for r in range(share):
-            white_ref[r, pl.ds(n, n_dev, stride=count), :] = rows_ref[:, r]
+            white_ref[r, pl.ds(n, n_dev, stride=count), :] = rows_ref[n_docs + n, :, r]
+    docs = jnp.concatenate(
+        [
+            jnp.concatenate([rows_ref[d, :n_dp, r] for d in range(n_docs)], axis=0)
+            for r in range(share)
+        ],
+        axis=1,
+    )
     white = jnp.concatenate([white_ref[r] for r in range(share)], axis=1).astype(bf16)
-    part = block_ref[:, n_docs + count].astype(f32)
-    rows_ref[:n_dp] = part.reshape(n_dp, n_seq, share, wg)[:, 0]
     each = n_docs // share
     owners = []
     for d in range(n_docs):
         lane = d % each * (wg // each)
-        column = rows_ref[:n_dp, d // each][:, lane : lane + 1]
+        column = rows_ref[n_docs + count, :n_dp, d // each][:, lane : lane + 1]
         owners.append(jnp.broadcast_to(column, (n_dp, n_dev * count)))
     upper = docs.astype(bf16)
     lower = (docs - upper.astype(f32)).astype(bf16)
@@ -381,7 +392,7 @@
             pltpu.VMEM((wa * count, wg), f32),
             pltpu.VMEM((activations.shape[0], wa), f32),
             pltpu.VMEM((activations.shape[0], wg), f32),
-            pltpu.VMEM((height, n_dev, wg), f32),
+            pltpu.VMEM((share * max(n_docs, count), n_dev, wg), f32),
             pltpu.SemaphoreType.DMA((7,)),
             pltpu.SemaphoreType.DMA((steps, 4)),
         ],
@@ -402,7 +413,7 @@
         in_specs=[vmem],
         out_specs=vmem,
         scratch_shapes=[
-            pltpu.VMEM((n_dev, share, wg), f32),
+            pltpu.VMEM((height // share, n_dev, share, wg), f32),
             pltpu.VMEM((share, n_dev * count, wg), f32),
         ],
         compiler_params=pltpu.CompilerParams(vmem_limit_bytes=small_bytes),

time: 32.2 us -> 32.1 us (level)
  no operation moved by 1% of the time
where the time goes in v6:
time: 32.1 us; the launch traced here: 32 us
  blocking collectives  24.7 us (77%)
  Pallas kernels  7.22 us (22%)
    all_to_all x1, blocking collectives, by_features(): blocks = everywhere(blocks)  15.5 us
    all_to_all x1, blocking collectives, by_features(): parts = everywhere(parts.reshape(n_dev, n_hi, 128))  9.19 us
    pallas_call x1, Pallas kernels, by_features(): pl.pallas_call(functools.partial(features_kernel, steps), out_shape=jax.S...  6 us
    pallas_call x1, Pallas kernels, by_features(): pl.pallas_call(finish_kernel, out_shape=jax.ShapeDtypeStruct((n_dp, n_out...  0.7 us

profile of v6, /device:TPU:0, one launch (start us, length us, event | category | flops | bytes accessed | tf_op | source)
XLA Modules:
  0.0 32.0 jit_solution(17301866977090150906)
XLA Ops:
  0.0 6.0 %features.1 = bf16[32,9,2,128]{3,2,1,0:T(2,128)(2,1)S(1)} custom-call(f32[4,8192]{1,0:T(4,128)} %refs_0_.1, f32[64,64]{1,0:T(8,128)} %refs_1_.1, f32[128,128]{1,0:T(8,128)} %refs_2_.1, f32[64,128]{1,0:T(8,128)} %refs_3_.1, s32[1,4,4]{2,1,0:T(4,128)} %refs_4_.1, s32[1,4]{1,0:T(1,128)} %refs_5_.1, s32[1,4]{1,0:T(1,128)} %refs_6_.1, bf16[512,5120]{1,0:T(8,128)(2,1)} %refs_7_.1, ...), custom_call_target="tpu_custom_call" | custom-call | tf_op jit(solution)/shard_map/features/pallas_call | solution.py:385
  6.0 15.5 %all_to_all.10.block_ref = bf16[32,9,2,128]{3,2,1,0:T(2,128)(2,1)S(1)} all-to-all(bf16[32,9,2,128]{3,2,1,0:T(2,128)(2,1)S(1)} %features.1), channel_id=1, replica_groups=mesh['dp'=8,'seq'=4] {'dp','seq'}, dimensions={0} | all-to-all | bytes 294912 | tf_op jit(solution)/shard_map/all_to_all | solution.py:409
  21.5 0.5 %partial.1 = f32[8,4,2,128]{3,2,1,0:T(2,128)S(1)} custom-call(bf16[32,9,2,128]{3,2,1,0:T(2,128)(2,1)S(1)} %all_to_all.10.block_ref), custom_call_target="tpu_custom_call" | custom-call | tf_op jit(solution)/shard_map/partial/pallas_call | solution.py:410
  22.1 9.2 %all_to_all.11.parts_ref = f32[32,2,128]{2,1,0:T(2,128)S(1)} all-to-all(f32[32,2,128]{2,1,0:T(2,128)S(1)} %bitcast.2), channel_id=1, replica_groups=mesh['dp'=8,'seq'=4] {'dp','seq'}, dimensions={0} | all-to-all | bytes 65536 | tf_op jit(solution)/shard_map/all_to_all | solution.py:422
  31.3 0.7 %finish.1 = f32[8,32]{1,0:T(8,128)} custom-call(f32[32,2,128]{2,1,0:T(2,128)S(1)} %all_to_all.11.parts_ref), custom_call_target="tpu_custom_call" | custom-call | tf_op jit(solution)/shard_map/finish/pallas_call | solution.py:423

commit v7 on v6

--- a/solution.py
+++ b/solution.py
@@ -198,7 +198,7 @@
             pltpu.make_async_copy(
                 hbm_refs[7 + i].at[:, cols], local_refs[7 + i].at[k], sems.at[k, i]
             )
-            for i in (2, 0, 3, 1)
+            for i in range(4)
         ]
 
     small = []
@@ -259,7 +259,8 @@
         target = jnp.where(place == d, owner[0, d], target)
     target = jnp.broadcast_to(target.astype(f32)[None], (n_dev, share, wg))
     out_ref[:, n_docs + count] = target.astype(bf16)
-    lax.fori_loop(0, steps, add_chunk, 0)
+    lax.fori_loop(0, steps - 1, add_chunk, 0)
+    add_chunk(steps - 1, 0)
     a_part = a_sum[...].T.astype(bf16).astype(f32)
     g_part = g_sum[...].astype(bf16)
     me = lax.axis_index("seq")

time: 32.1 us -> 32 us (level)
  no operation moved by 1% of the time
where the time goes in v7:
time: 32 us; the launch traced here: 31.8 us
  blocking collectives  24.7 us (77%)
  Pallas kernels  7.08 us (22%)
    all_to_all x1, blocking collectives, by_features(): blocks = everywhere(blocks)  15.5 us
    all_to_all x1, blocking collectives, by_features(): parts = everywhere(parts.reshape(n_dev, n_hi, 128))  9.19 us
    pallas_call x1, Pallas kernels, by_features(): pl.pallas_call(functools.partial(features_kernel, steps), out_shape=jax.S...  5.86 us
    pallas_call x1, Pallas kernels, by_features(): pl.pallas_call(finish_kernel, out_shape=jax.ShapeDtypeStruct((n_dp, n_out...  0.7 us

profile of v7, /device:TPU:0, one launch (start us, length us, event | category | flops | bytes accessed | tf_op | source)
XLA Modules:
  0.0 31.8 jit_solution(11632357127950431707)
XLA Ops:
  0.0 5.9 %features.1 = bf16[32,9,2,128]{3,2,1,0:T(2,128)(2,1)S(1)} custom-call(f32[4,8192]{1,0:T(4,128)} %refs_0_.1, f32[64,64]{1,0:T(8,128)} %refs_1_.1, f32[128,128]{1,0:T(8,128)} %refs_2_.1, f32[64,128]{1,0:T(8,128)} %refs_3_.1, s32[1,4,4]{2,1,0:T(4,128)} %refs_4_.1, s32[1,4]{1,0:T(1,128)} %refs_5_.1, s32[1,4]{1,0:T(1,128)} %refs_6_.1, bf16[512,5120]{1,0:T(8,128)(2,1)} %refs_7_.1, ...), custom_call_target="tpu_custom_call" | custom-call | tf_op jit(solution)/shard_map/features/pallas_call | solution.py:386
  5.9 15.5 %all_to_all.10.block_ref = bf16[32,9,2,128]{3,2,1,0:T(2,128)(2,1)S(1)} all-to-all(bf16[32,9,2,128]{3,2,1,0:T(2,128)(2,1)S(1)} %features.1), channel_id=1, replica_groups=mesh['dp'=8,'seq'=4] {'dp','seq'}, dimensions={0} | all-to-all | bytes 294912 | tf_op jit(solution)/shard_map/all_to_all | solution.py:410
  21.4 0.5 %partial.1 = f32[8,4,2,128]{3,2,1,0:T(2,128)S(1)} custom-call(bf16[32,9,2,128]{3,2,1,0:T(2,128)(2,1)S(1)} %all_to_all.10.block_ref), custom_call_target="tpu_custom_call" | custom-call | tf_op jit(solution)/shard_map/partial/pallas_call | solution.py:411
  21.9 9.2 %all_to_all.11.parts_ref = f32[32,2,128]{2,1,0:T(2,128)S(1)} all-to-all(f32[32,2,128]{2,1,0:T(2,128)S(1)} %bitcast.2), channel_id=1, replica_groups=mesh['dp'=8,'seq'=4] {'dp','seq'}, dimensions={0} | all-to-all | bytes 65536 | tf_op jit(solution)/shard_map/all_to_all | solution.py:423
  31.1 0.7 %finish.1 = f32[8,32]{1,0:T(8,128)} custom-call(f32[32,2,128]{2,1,0:T(2,128)S(1)} %all_to_all.11.parts_ref), custom_call_target="tpu_custom_call" | custom-call | tf_op jit(solution)/shard_map/finish/pallas_call | solution.py:424

commit v8 on v7

--- a/solution.py
+++ b/solution.py
@@ -336,13 +336,13 @@
             [scores[lo * tall : (lo + 1) * tall, lanes] for lo in range(n_lo)], axis=1
         )
         for hi in range(n_hi):
-            out_ref[:, s, hi, :] = packed[hi * n_dp : (hi + 1) * n_dp]
+            out_ref[:, s, hi, :] = packed[hi * n_dp : (hi + 1) * n_dp].astype(bf16)
 
 
 def finish_kernel(parts_ref, out_ref):
     n_hi = parts_ref.shape[1]
     n_dp, n_out = out_ref.shape
-    total = jnp.sum(parts_ref[...], axis=0)
+    total = jnp.sum(parts_ref[...].astype(jnp.float32), axis=0)
     for lo in range(n_dp // n_hi):
         out_ref[lo * n_hi : (lo + 1) * n_hi, :] = total[:, lo * n_out : (lo + 1) * n_out]
 
@@ -410,7 +410,7 @@
     blocks = everywhere(blocks)
     parts = pl.pallas_call(
         functools.partial(partial_kernel, n_docs),
-        out_shape=jax.ShapeDtypeStruct((n_dp, n_seq, n_hi, 128), f32),
+        out_shape=jax.ShapeDtypeStruct((n_dp, n_seq, n_hi, 128), bf16),
         in_specs=[vmem],
         out_specs=vmem,
         scratch_shapes=[

time: 32 us -> 31.9 us (level)
  no operation moved by 1% of the time
where the time goes in v8:
time: 31.9 us; the launch traced here: 31.7 us
  blocking collectives  24.6 us (77%)
  Pallas kernels  7.08 us (22%)
    all_to_all x1, blocking collectives, by_features(): blocks = everywhere(blocks)  15.5 us
    all_to_all x1, blocking collectives, by_features(): parts = everywhere(parts.reshape(n_dev, n_hi, 128))  9.09 us
    pallas_call x1, Pallas kernels, by_features(): pl.pallas_call(functools.partial(features_kernel, steps), out_shape=jax.S...  5.86 us
    pallas_call x1, Pallas kernels, by_features(): pl.pallas_call(finish_kernel, out_shape=jax.ShapeDtypeStruct((n_dp, n_out...  0.7 us

profile of v8, /device:TPU:0, one launch (start us, length us, event | category | flops | bytes accessed | tf_op | source)
XLA Modules:
  0.0 31.7 jit_solution(11922575108678404185)
XLA Ops:
  0.0 5.9 %features.1 = bf16[32,9,2,128]{3,2,1,0:T(2,128)(2,1)S(1)} custom-call(f32[4,8192]{1,0:T(4,128)} %refs_0_.1, f32[64,64]{1,0:T(8,128)} %refs_1_.1, f32[128,128]{1,0:T(8,128)} %refs_2_.1, f32[64,128]{1,0:T(8,128)} %refs_3_.1, s32[1,4,4]{2,1,0:T(4,128)} %refs_4_.1, s32[1,4]{1,0:T(1,128)} %refs_5_.1, s32[1,4]{1,0:T(1,128)} %refs_6_.1, bf16[512,5120]{1,0:T(8,128)(2,1)} %refs_7_.1, ...), custom_call_target="tpu_custom_call" | custom-call | tf_op jit(solution)/shard_map/features/pallas_call | solution.py:386
  5.9 15.5 %all_to_all.10.block_ref = bf16[32,9,2,128]{3,2,1,0:T(2,128)(2,1)S(1)} all-to-all(bf16[32,9,2,128]{3,2,1,0:T(2,128)(2,1)S(1)} %features.1), channel_id=1, replica_groups=mesh['dp'=8,'seq'=4] {'dp','seq'}, dimensions={0} | all-to-all | bytes 294912 | tf_op jit(solution)/shard_map/all_to_all | solution.py:410
  21.4 0.5 %partial.1 = bf16[8,4,2,128]{3,2,1,0:T(2,128)(2,1)S(1)} custom-call(bf16[32,9,2,128]{3,2,1,0:T(2,128)(2,1)S(1)} %all_to_all.10.block_ref), custom_call_target="tpu_custom_call" | custom-call | tf_op jit(solution)/shard_map/partial/pallas_call | solution.py:411
  21.9 9.1 %all_to_all.11.parts_ref = bf16[32,2,128]{2,1,0:T(2,128)(2,1)S(1)} all-to-all(bf16[32,2,128]{2,1,0:T(2,128)(2,1)S(1)} %bitcast.2), channel_id=1, replica_groups=mesh['dp'=8,'seq'=4] {'dp','seq'}, dimensions={0} | all-to-all | bytes 32768 | tf_op jit(solution)/shard_map/all_to_all | solution.py:423
  31.0 0.7 %finish.1 = f32[8,32]{1,0:T(8,128)} custom-call(bf16[32,2,128]{2,1,0:T(2,128)(2,1)S(1)} %all_to_all.11.parts_ref), custom_call_target="tpu_custom_call" | custom-call | tf_op jit(solution)/shard_map/finish/pallas_call | solution.py:424
